TPU v7x, 512 devices: a whole 4x4x16 slice. The times are simulated.
512 devices in a mesh: row: 8 (over y, core), col: 32 (over z_lo, x), grp: 2 (over z_hi).
Axes of the slice: x: 4, y: 4, z: 16 (z_hi: 2, z_lo: 8; z = z_hi * 8 + z_lo), core: 2. Of those that a mesh axis runs over, the one named last changes fastest.
Arguments:
- momentum: float32 [2, 4096, 16384], P('grp', 'row', 'col'), may hold values from -6 to 6
- gradient: bfloat16 [2, 4096, 16384], P('grp', 'row', 'col'), may hold values from -6 to 6
- factor_q: float32 [2, 16384, 256], P('grp', 'col', 'row'), may hold values from -0.046875 to 0.046875
- weights: float32 [2, 4096, 16384], P(None, 'row', ('col', 'grp')), may hold values from -6 to 6
- tokens: bfloat16 [256, 4096], P(None, 'row'), may hold values from -0.08984375 to 0.08984375
Outputs:
- momentum_out: float32 [2, 4096, 16384], P('grp', 'row', 'col')
- factor_out: float32 [2, 16384, 256], P('grp', 'col', 'row')
- weights_out: float32 [2, 4096, 16384], P(None, 'row', ('col', 'grp'))
- hidden: bfloat16 [256, 16384], P('row', ('col', 'grp'))
All inputs are finite; a program needn't handle non-finite values.
Results may differ from a plain program's by a relative error of at most 0.0061.
Values may be sent and summed in bfloat16 or wider, within the bound.
A program may use at most 64 MiB of HBM per device.

v0:
```python
import math

import jax
import jax.numpy as jnp
from jax import lax
from jax.sharding import PartitionSpec as P

D = 4096
HID = 16384


feedback = 0.05
epsilon = 1e-06


def sent_to_all(value, axis):
    copies = jnp.broadcast_to(value, (lax.axis_size(axis), *value.shape))
    return lax.all_to_all(copies, axis, split_axis=0, concat_axis=0, tiled=True)


def in_order(blocks, dim):
    lengths = list(blocks.shape[1:])
    lengths[dim] *= blocks.shape[0]
    return jnp.moveaxis(blocks, 0, dim).reshape(lengths)


def gather_directly(value, axis, dim):
    blocks = sent_to_all(value, axis)
    return in_order(blocks, dim)


def split_up(value, dim, size):
    before, after = (value.shape[:dim], value.shape[dim + 1 :])
    return jnp.moveaxis(value.reshape(*before, size, -1, *after), dim, 0)


def summed_on_arrival(value, axis, dim):
    size = lax.axis_size(axis)
    blocks = lax.all_to_all(split_up(value, dim, size), axis, 0, 0, tiled=True)
    return jnp.sum(blocks, axis=0)


def padded_to(lines, size):
    spare = -len(lines) % size
    return jnp.pad(lines, [(0, spare)] + [(0, 0)] * (lines.ndim - 1))


def nested_sum(value, axes):
    lines = value.reshape(-1, value.shape[-1])
    own = summed_on_arrival(padded_to(lines, lax.axis_size(axes)), axes, 0)
    whole = gather_directly(own, axes, 0)
    return whole[: len(lines)].reshape(value.shape)


def taken_together(value, axis):
    everything = sent_to_all(value, axis)
    return jnp.sum(everything, axis=0)


def rows_first(arrays, axis, dims):
    turned = [jnp.moveaxis(a, dim, 0) for a, dim in zip(arrays, dims)]
    widths = [t[0].size for t in turned]
    both = jnp.concatenate([t.reshape(-1, w) for t, w in zip(turned, widths)], axis=1)
    whole = lax.all_gather(both, axis, axis=0, tiled=True)
    blocks = jnp.split(whole, [sum(widths[:k]) for k in range(1, len(widths))], axis=1)
    return tuple(
        (
            jnp.moveaxis(b.reshape(-1, *t.shape[1:]), 0, dim)
            for b, t, dim in zip(blocks, turned, dims)
        )
    )


def gram_of(left_rows):
    return jnp.dot(left_rows.T, left_rows, precision=lax.Precision.HIGHEST)


def orthonormal(gram_sum, left_rows):
    factor_l = jnp.linalg.cholesky(gram_sum)
    return jax.scipy.linalg.solve_triangular(factor_l, left_rows.T, lower=True).T


def local(momentum, gradient, factor_q, weights, tokens):
    buffer = momentum[0] + gradient[0].astype(jnp.float32)
    buffer_h = buffer.astype(jnp.bfloat16)
    partial_value = jnp.dot(
        buffer_h,
        gather_directly(factor_q[0].astype(jnp.bfloat16), "row", 1),
        preferred_element_type=jnp.float32,
    )
    left_full = nested_sum(partial_value, "col")
    gram_sum = taken_together(gram_of(left_full), "row")
    left_h = orthonormal(gram_sum, left_full).astype(jnp.bfloat16)
    right_part = lax.dot_general(
        buffer_h, left_h, (((0,), (0,)), ((), ())), preferred_element_type=jnp.float32
    )
    right_share = summed_on_arrival(right_part, "row", 1)
    squares = taken_together(jnp.sum(right_share * right_share, axis=0), "col")
    q_share = right_share / jnp.sqrt(squares + epsilon)
    right_h, new_q_h = rows_first(
        (right_share.astype(jnp.bfloat16), q_share.astype(jnp.bfloat16)), "row", (1, 1)
    )
    feedback_term = lax.dot_general(
        left_h, right_h, (((1,), (1,)), ((), ())), preferred_element_type=jnp.float32
    )
    mom_new = buffer - feedback * feedback_term
    left_both = gather_directly(left_h[None], "grp", 0)
    right_both = lax.all_to_all(new_q_h[None], "grp", split_axis=1, concat_axis=0, tiled=True)
    step_size = 0.4 * math.sqrt(max(D, HID))
    low_rank = lax.dot_general(
        left_both, right_both, (((2,), (2,)), ((0,), (0,))), preferred_element_type=jnp.float32
    )
    new_weights = weights - step_size * low_rank
    weights_h = new_weights.astype(jnp.bfloat16)
    dec_parts = summed_on_arrival(
        jnp.einsum("bd,pdh->bph", tokens, weights_h, preferred_element_type=jnp.float32), "row", 0
    )
    hidden = (jax.nn.silu(dec_parts[:, 0]) * dec_parts[:, 1]).astype(jnp.bfloat16)
    return (mom_new[None], q_share[None], new_weights, hidden)


def solution(mesh):
    in_specs = (
        P("grp", "row", "col"),
        P("grp", "row", "col"),
        P("grp", "col", "row"),
        P(None, "row", ("col", "grp")),
        P(None, "row"),
    )
    out_specs = (
        P("grp", "row", "col"),
        P("grp", "col", "row"),
        P(None, "row", ("col", "grp")),
        P("row", ("col", "grp")),
    )
    return jax.shard_map(local, mesh=mesh, in_specs=in_specs, out_specs=out_specs, check_vma=False)
```

profile of v0, /device:TPU:1, one launch (start us, length us, event | category | flops | bytes accessed | tf_op | source)
XLA Modules:
  0.0 311.4 jit_solution(5631306056553936782)
XLA Ops:
  0.6 0.9 convert_bitcast_fusion.1
  2.3 10.2 %all-to-all-start = ((bf16[8,512,32]{1,2,0:T(8,128)(2,1)}), bf16[8,512,32]{1,2,0:T(8,128)(2,1)S(1)}, u32[]{:S(2)}, u32[]{:S(2)}) async-start(bf16[8,512,32]{1,2,0:T(8,128)(2,1)} %broadcast_in_dim.26), calls=%async_computation | async-start | bytes 524288 | tf_op jit(solution)/shard_map/all_to_all | solution.py:18
  12.5 1.5 fusion.3
  14.0 5.0 %all-to-all-done = bf16[8,512,32]{1,2,0:T(8,128)(2,1)S(1)} async-done(((bf16[8,512,32]{1,2,0:T(8,128)(2,1)}), bf16[8,512,32]{1,2,0:T(8,128)(2,1)S(1)}, u32[]{:S(2)}, u32[]{:S(2)}) %all-to-all-start) | async-done | bytes 262176 | tf_op jit(solution)/shard_map/all_to_all | solution.py:18
  19.3 37.4 %all_to_all.53 = f32[32,16,256]{2,1,0:T(8,128)S(1)} all-to-all(f32[32,16,256]{2,1,0:T(8,128)S(1)} %fusion.22), channel_id=1, replica_groups=mesh['row'=8,'col'=32,'grp'=2] {'col'}, dimensions={0} | all-to-all | bytes 1048576 | tf_op jit(solution)/shard_map/all_to_all | solution.py:39
  56.8 35.3 %all_to_all.54 = f32[32,16,256]{2,1,0:T(8,128)S(1)} all-to-all(f32[32,16,256]{2,1,0:T(8,128)S(1)} %broadcast_in_dim.27), channel_id=1, replica_groups=mesh['row'=8,'col'=32,'grp'=2] {'col'}, dimensions={0} | all-to-all | bytes 1048576 | tf_op jit(solution)/shard_map/all_to_all | solution.py:18
  92.1 1.0 convolution_bitcast_fusion.1
  93.2 1.5 broadcast_in_dim.28
  94.7 7.4 %all-to-all-start.3 = ((f32[8,256,256]{2,1,0:T(8,128)}), f32[8,256,256]{2,1,0:T(8,128)S(1)}, u32[]{:S(2)}, u32[]{:S(2)}) async-start(f32[8,256,256]{2,1,0:T(8,128)} %broadcast_in_dim.28), calls=%async_computation.3 | async-start | bytes 4194304 | tf_op jit(solution)/shard_map/all_to_all | solution.py:18
  102.3 26.1 %all-to-all-done.3 = f32[8,256,256]{2,1,0:T(8,128)S(1)} async-done(((f32[8,256,256]{2,1,0:T(8,128)}), f32[8,256,256]{2,1,0:T(8,128)S(1)}, u32[]{:S(2)}, u32[]{:S(2)}) %all-to-all-start.3) | async-done | bytes 2097184 | tf_op jit(solution)/shard_map/all_to_all | solution.py:18
  128.7 11.7 %cholesky.50 = f32[128,128]{1,0:T(8,128)S(1)} custom-call(f32[128,128]{1,0:T(8,128)S(1)} %cholesky.118), custom_call_target="Cholesky" | custom-call | tf_op jit(solution)/shard_map/jit(cholesky)/cholesky | solution.py:79
  140.5 9.8 %custom-call.15 = f32[1,128,128]{1,2,0:T(8,128)S(1)} custom-call(f32[1,128,128]{2,1,0:T(8,128)S(1)} %get-tuple-element.35), custom_call_target="InvertDiagBlocksLowerTriangular" | custom-call | tf_op jit(solution)/shard_map/jit(cholesky)/cholesky | solution.py:79
  150.8 11.7 %cholesky.105 = f32[128,128]{1,0:T(8,128)S(1)} custom-call(f32[128,128]{1,0:T(8,128)S(1)} %convolution_subtract_fusion.1), custom_call_target="Cholesky" | custom-call | tf_op jit(solution)/shard_map/jit(cholesky)/cholesky | solution.py:79
  164.6 4.0 %while.1 = (s32[]{:T(128)}, f32[256,256]{1,0:T(8,128)S(1)}, s32[2,2]{1,0:T(2,128)S(1)}, f32[2,128,128]{2,1,0:T(8,128)S(1)}, s32[]{:T(128)}) while((s32[]{:T(128)}, f32[256,256]{1,0:T(8,128)S(1)}, s32[2,2]{1,0:T(2,128)S(1)}, f32[2,128,128]{2,1,0:T(8,128)S(1)}, s32[]{:T(128)}) %tuple.30), condition=%wide.while_cond, body=%wide.while_body.sunk | while | flops 2 | bytes 131181 | solution.py:80
  165.2 1.4 bitcast_dynamic-update-slice_fusion.2
  167.2 1.4 bitcast_dynamic-update-slice_fusion.2
  168.6 19.9 %custom-call.16 = f32[2,128,128]{1,2,0:T(8,128)S(1)} custom-call(f32[2,128,128]{2,1,0:T(8,128)S(1)} %get-tuple-element.11), custom_call_target="InvertDiagBlocksLowerTriangular" | custom-call | tf_op jit(solution)/shard_map/jit(_solve_triangular)/triangular_solve | solution.py:80
  190.5 12.6 %all_to_all.55 = f32[8,512,32]{1,2,0:T(8,128)S(1)} all-to-all(f32[8,512,32]{1,2,0:T(8,128)S(1)} %convolution_bitcast_fusion), channel_id=1, replica_groups=mesh['row'=8,'col'=32,'grp'=2] {'row'}, dimensions={0} | all-to-all | bytes 1048576 | tf_op jit(solution)/shard_map/all_to_all | solution.py:39
  203.3 17.0 %all_to_all.56 = f32[32,1,32]{2,1,0:T(1,128)S(1)} all-to-all(f32[32,1,32]{2,1,0:T(1,128)S(1)} %broadcast_in_dim.29), channel_id=1, replica_groups=mesh['row'=8,'col'=32,'grp'=2] {'col'}, dimensions={0} | all-to-all | bytes 8192 | tf_op jit(solution)/shard_map/all_to_all | solution.py:18
  220.5 15.4 %all_gather.3 = bf16[256,1024]{1,0:T(8,128)(2,1)S(1)} all-gather(bf16[32,1024]{1,0:T(8,128)(2,1)S(1)} %pad_maximum_fusion), channel_id=1, replica_groups=mesh['row'=8,'col'=32,'grp'=2] {'row'}, dimensions={0}, use_global_device_ids=true | all-gather | bytes 589824 | tf_op jit(solution)/shard_map/all_gather | solution.py:64
  237.0 2.2 reduce.13
  239.2 0.8 reshape.120
  239.9 7.3 %all-to-all-start.7 = ((bf16[2,2,32768]{2,1,0:T(2,128)(2,1)}), bf16[2,2,32768]{2,1,0:T(2,128)(2,1)S(1)}, u32[]{:S(2)}, u32[]{:S(2)}) async-start(bf16[2,2,32768]{2,1,0:T(2,128)(2,1)} %reshape.120), calls=%async_computation.7 | async-start | bytes 524288 | tf_op jit(solution)/shard_map/all_to_all | solution.py:108
  247.4 13.4 %all-to-all-done.7 = bf16[2,2,32768]{2,1,0:T(2,128)(2,1)S(1)} async-done(((bf16[2,2,32768]{2,1,0:T(2,128)(2,1)}), bf16[2,2,32768]{2,1,0:T(2,128)(2,1)S(1)}, u32[]{:S(2)}, u32[]{:S(2)}) %all-to-all-start.7) | async-done | bytes 262176 | tf_op jit(solution)/shard_map/all_to_all | solution.py:108
  260.8 0.8 broadcast_in_dim.31
  261.6 3.5 %all-to-all-start.6 = ((bf16[2,1,512,256]{3,2,1,0:T(8,128)(2,1)}), bf16[2,1,512,256]{3,2,1,0:T(8,128)(2,1)S(1)}, u32[]{:S(2)}, u32[]{:S(2)}) async-start(bf16[2,1,512,256]{3,2,1,0:T(8,128)(2,1)} %broadcast_in_dim.31), calls=%async_computation.6 | async-start | bytes 1048576 | tf_op jit(solution)/shard_map/all_to_all | solution.py:18
  265.5 14.1 %all-to-all-done.6 = bf16[2,1,512,256]{3,2,1,0:T(8,128)(2,1)S(1)} async-done(((bf16[2,1,512,256]{3,2,1,0:T(8,128)(2,1)}), bf16[2,1,512,256]{3,2,1,0:T(8,128)(2,1)S(1)}, u32[]{:S(2)}, u32[]{:S(2)}) %all-to-all-start.6) | async-done | bytes 524320 | tf_op jit(solution)/shard_map/all_to_all | solution.py:18
  279.5 1.6 fusion
  281.4 0.8 copy.54
  282.3 19.0 %all-to-all-start.8 = ((f32[8,32,2,256]{3,1,2,0:T(8,128)}), f32[8,32,2,256]{3,1,2,0:T(8,128)S(1)}, u32[]{:S(2)}, u32[]{:S(2)}) async-start(f32[8,32,2,256]{3,1,2,0:T(8,128)} %copy.54), calls=%async_computation.8 | async-start | bytes 1048576 | tf_op jit(solution)/shard_map/all_to_all | solution.py:39
  301.2 2.4 fusion.2
  304.4 6.4 %all-to-all-done.8 = f32[8,32,2,256]{3,1,2,0:T(8,128)S(1)} async-done(((f32[8,32,2,256]{3,1,2,0:T(8,128)}), f32[8,32,2,256]{3,1,2,0:T(8,128)S(1)}, u32[]{:S(2)}, u32[]{:S(2)}) %all-to-all-start.8) | async-done | bytes 524320 | tf_op jit(solution)/shard_map/all_to_all | solution.py:39
  (59 shorter events, 9.6 us)
Async XLA Ops:
  0.6 280.5 %copy-start = (bf16[256,512]{1,0:T(8,128)(2,1)S(1)}, bf16[256,512]{1,0:T(8,128)(2,1)}, u32[]{:S(2)}) copy-start(bf16[256,512]{1,0:T(8,128)(2,1)} %param.9) | copy-start | bytes 786436
  2.3 16.7 %all-to-all-start = ((bf16[8,512,32]{1,2,0:T(8,128)(2,1)}), bf16[8,512,32]{1,2,0:T(8,128)(2,1)S(1)}, u32[]{:S(2)}, u32[]{:S(2)}) async-start(bf16[8,512,32]{1,2,0:T(8,128)(2,1)} %broadcast_in_dim.26), calls=%async_computation | async-start | bytes 524288 | tf_op jit(solution)/shard_map/all_to_all | solution.py:18
  14.0 5.0 %copy-start.3 = (bf16[1,512,512]{2,1,0:T(8,128)(2,1)}, bf16[1,512,512]{2,1,0:T(8,128)(2,1)S(1)}, u32[]{:S(2)}) copy-start(bf16[1,512,512]{2,1,0:T(8,128)(2,1)S(1)} %fusion.3) | copy-start | bytes 1572868
  94.7 33.7 %all-to-all-start.3 = ((f32[8,256,256]{2,1,0:T(8,128)}), f32[8,256,256]{2,1,0:T(8,128)S(1)}, u32[]{:S(2)}, u32[]{:S(2)}) async-start(f32[8,256,256]{2,1,0:T(8,128)} %broadcast_in_dim.28), calls=%async_computation.3 | async-start | bytes 4194304 | tf_op jit(solution)/shard_map/all_to_all | solution.py:18
  150.8 39.0 %copy-start.4 = (bf16[1,512,512]{2,1,0:T(8,128)(2,1)S(1)}, bf16[1,512,512]{2,1,0:T(8,128)(2,1)}, u32[]{:S(2)}) copy-start(bf16[1,512,512]{2,1,0:T(8,128)(2,1)} %copy-done.3) | copy-start | bytes 1572868
  189.8 0.7 copy-start.5
  239.9 20.9 %all-to-all-start.7 = ((bf16[2,2,32768]{2,1,0:T(2,128)(2,1)}), bf16[2,2,32768]{2,1,0:T(2,128)(2,1)S(1)}, u32[]{:S(2)}, u32[]{:S(2)}) async-start(bf16[2,2,32768]{2,1,0:T(2,128)(2,1)} %reshape.120), calls=%async_computation.7 | async-start | bytes 524288 | tf_op jit(solution)/shard_map/all_to_all | solution.py:108
  261.6 17.9 %all-to-all-start.6 = ((bf16[2,1,512,256]{3,2,1,0:T(8,128)(2,1)}), bf16[2,1,512,256]{3,2,1,0:T(8,128)(2,1)S(1)}, u32[]{:S(2)}, u32[]{:S(2)}) async-start(bf16[2,1,512,256]{3,2,1,0:T(8,128)(2,1)} %broadcast_in_dim.31), calls=%async_computation.6 | async-start | bytes 1048576 | tf_op jit(solution)/shard_map/all_to_all | solution.py:18
  281.1 22.6 %copy-start.2 = (f32[2,512,256]{2,1,0:T(8,128)}, f32[2,512,256]{2,1,0:T(8,128)S(1)}, u32[]{:S(2)}) copy-start(f32[2,512,256]{2,1,0:T(8,128)S(1)} %fusion) | copy-start | bytes 3145732
  281.1 20.1 %copy-start.1 = (f32[1,512,512]{2,1,0:T(8,128)S(1)}, f32[1,512,512]{2,1,0:T(8,128)}, u32[]{:S(2)}) copy-start(f32[1,512,512]{2,1,0:T(8,128)} %param.5) | copy-start | bytes 3145732
  282.3 28.5 %all-to-all-start.8 = ((f32[8,32,2,256]{3,1,2,0:T(8,128)}), f32[8,32,2,256]{3,1,2,0:T(8,128)S(1)}, u32[]{:S(2)}, u32[]{:S(2)}) async-start(f32[8,32,2,256]{3,1,2,0:T(8,128)} %copy.54), calls=%async_computation.8 | async-start | bytes 1048576 | tf_op jit(solution)/shard_map/all_to_all | solution.py:39
where the time goes:
time: 315 us; the launch traced here: 311 us
  blocking collectives  118 us (37%)
  waiting for transfers between devices  65 us (21%)
  other arithmetic  60.4 us (19%)
  starting transfers between devices  47.3 us (15%)
  local copies, waits for them, and re-layouts  11 us (3%)
  matrix products  7.59 us (2%)
    all_to_all x2, blocking collectives, sent_to_all(): return lax.all_to_all(copies, axis, split_axis=0, concat_axis=0, tiled=True)  52.4 us
    all_to_all x2, blocking collectives, summed_on_arrival(): blocks = lax.all_to_all(split_up(value, dim, size), axis, 0, 0, tiled=True)  50 us
    all_to_all x3, waiting for transfers between devices, sent_to_all(): return lax.all_to_all(copies, axis, split_axis=0, concat_axis=0, tiled=True)  45.2 us
    another operation x6, other arithmetic, orthonormal(): factor_l = jnp.linalg.cholesky(gram_sum)  33.9 us
    all_to_all x3, starting transfers between devices, sent_to_all(): return lax.all_to_all(copies, axis, split_axis=0, concat_axis=0, tiled=True)  21 us
    another operation x3, other arithmetic, orthonormal(): jax.scipy.linalg.solve_triangular(factor_l, left_rows.T, lower=True)  19.9 us
    all_to_all x1, starting transfers between devices, summed_on_arrival(): blocks = lax.all_to_all(split_up(value, dim, size), axis, 0, 0, tiled=True)  19 us
    all_gather x1, blocking collectives, rows_first(): whole = lax.all_gather(both, axis, axis=0, tiled=True)  15.4 us
  transfers between devices with their start and end apart: 5, of which 5 were waited for; matrix products, arithmetic and copies ran while one was open for 2% of the time, Pallas kernels for 0%

commit v1 on v0

v1 whole, which is shorter than its diff:
```python
import functools
import math

import jax
import jax.numpy as jnp
from jax import lax
from jax.experimental import pallas as pl
from jax.experimental.pallas import tpu as pltpu
from jax.sharding import PartitionSpec as P

D = 4096
HID = 16384
RANK = 256
BATCH = 256
FEEDBACK = 0.05
EPSILON = 1e-06
STEP = 0.4 * math.sqrt(max(D, HID))
NX = 4

f32, bf16 = jnp.float32, jnp.bfloat16
HI = lax.Precision.HIGHEST
MESH = pl.DeviceIdType.MESH
NN = (((1,), (0,)), ((), ()))
NT = (((1,), (1,)), ((), ()))
TN = (((0,), (0,)), ((), ()))


def mm(a, b, dims=NN, precision=None):
    return lax.dot_general(a, b, dims, precision=precision, preferred_element_type=f32)


def wrap(i, d, n):
    return lax.rem(i + d, n)


class Place:
    def __init__(self, sizes):
        self.nr, self.nc, self.ng = sizes
        self.nx, self.nz = NX, self.nc // NX
        self.r, self.c, self.g = (lax.axis_index(a) for a in ("row", "col", "grp"))
        self.x, self.z = lax.rem(self.c, self.nx), lax.div(self.c, self.nx)

    def at(self, dr=0, dx=0, dz=0, dg=0):
        c = wrap(self.z, dz, self.nz) * self.nx + wrap(self.x, dx, self.nx)
        return (wrap(self.r, dr, self.nr), c, wrap(self.g, dg, self.ng))


def greet(partners):
    barrier = pltpu.get_barrier_semaphore()
    for device in partners:
        pl.semaphore_signal(barrier, inc=1, device_id=device, device_id_type=MESH)
    return lambda: pl.semaphore_wait(barrier, len(partners))


def send(src, dst, sems, k, device):
    copy = pltpu.make_async_remote_copy(
        src_ref=src, dst_ref=dst, send_sem=sems.at[0, k], recv_sem=sems.at[1, k], device_id=device, device_id_type=MESH
    )
    copy.start()
    return copy


def arrived(copies):
    for copy in copies:
        copy.wait_recv()


def left_kernel(sizes, mom, grad, fq, w, tok, left_o, gram_o, base_o,
                bufh, qbuf, part, rx, sx, rz, l512, gp, rg, gf, pre, rpre,
                s_q, s_x, s_z, s_az, s_ax, s_g, s_ag, s_p):
    at = Place(sizes)
    nr, nx, nz = at.nr, at.nx, at.nz
    plane = [(dx, dr) for dx in range(nx) for dr in range(nr) if dx or dr]
    ready = greet([at.at(dr=dr, dx=dx) for dx, dr in plane] + [at.at(dz=d) for d in range(1, nz)])
    r, x, z = at.r, at.x, at.z
    sent = []

    qbuf[r] = fq[...].T.astype(bf16)
    bufh[...] = (mom[...] + grad[...].astype(f32)).astype(bf16)
    ready()
    got_q = [send(qbuf.at[r], qbuf.at[r], s_q, d - 1, at.at(dr=d)) for d in range(1, nr)]
    for p in range(2):
        high = w[p].astype(bf16)
        low = (w[p] - high.astype(f32)).astype(bf16)
        pre[:, p] = (mm(tok[...], high) + mm(tok[...], low)).reshape(pre[:, p].shape)
    arrived(got_q)
    part[...] = mm(bufh[...], qbuf[...].reshape(RANK, -1), NT).reshape(part.shape)
    got_x = [send(part.at[wrap(x, d, nx)], rx.at[d - 1], s_x, d - 1, at.at(dx=d)) for d in range(1, nx)]
    got_p = [send(pre.at[wrap(r, d, nr)], rpre.at[d - 1], s_p, d - 1, at.at(dr=d)) for d in range(1, nr)]
    arrived(got_x)
    sx[...] = (part[x] + jnp.sum(rx[...], axis=0)).reshape(sx.shape)
    got_z = [send(sx.at[wrap(z, d, nz)], rz.at[d - 1], s_z, d - 1, at.at(dz=d)) for d in range(1, nz)]
    arrived(got_z)
    l512[x, z] = sx[z] + jnp.sum(rz[...], axis=0)
    got_az = [send(l512.at[x, z], l512.at[x, z], s_az, d - 1, at.at(dz=d)) for d in range(1, nz)]
    arrived(got_az)
    rows = l512[x].reshape(-1, RANK)
    gp[...] = mm(rows, rows, TN, HI).reshape(gp.shape)
    got_g = []
    for k, (dx, dr) in enumerate(plane):
        m = wrap(x, dx, nx) * nr + wrap(r, dr, nr)
        got_g.append(send(gp.at[m], rg.at[k], s_g, k, at.at(dr=dr, dx=dx)))
    got_ax = [send(l512.at[x], l512.at[x], s_ax, d - 1, at.at(dx=d)) for d in range(1, nx)]
    arrived(got_g)
    m = x * nr + r
    gf[m] = gp[m] + jnp.sum(rg[...], axis=0)
    got_ag = [send(gf.at[m], gf.at[m], s_ag, k, at.at(dr=dr, dx=dx)) for k, (dx, dr) in enumerate(plane)]
    arrived(got_p)
    base_o[...] = pre[r] + jnp.sum(rpre[...], axis=0)
    arrived(got_ax)
    left_o[...] = l512[...].reshape(left_o.shape)
    arrived(got_ag)
    gram_o[...] = gf[...].reshape(gram_o.shape)
    for copies in (got_q, got_x, got_p, got_z, got_az, got_g, got_ax, got_ag):
        for copy in copies:
            copy.wait_send()


def right_kernel(sizes, mom, grad, left, wt, w, base, tok, mom_o, fac_o, new_o, hid_o,
                 bufh, lh, oth, rt, rrt, tl, rtl, tls, tlo, rh, sho, rho, sq, rsq, nb,
                 s_l, s_rt, s_tl, s_lz, s_lx, s_rh, s_sh, s_ro, s_sq, s_nb, s_to):
    at = Place(sizes)
    nr, nx, nz, ng = at.nr, at.nx, at.nz, at.ng
    r, c, g, x, z = at.r, at.c, at.g, at.x, at.z
    column = [(dg, dz, dx) for dg in range(ng) for dz in range(nz) for dx in range(nx) if dg or dz or dx]
    ready = greet([at.at(dr=d) for d in range(1, nr)] + [at.at(dg=dg, dz=dz, dx=dx) for dg, dz, dx in column])
    o = 1 - g
    kr = RANK // nr
    half = w.shape[2]

    buffer = mom[...] + grad[...].astype(f32)
    bufh[...] = buffer.astype(bf16)
    left_h = mm(left[...], wt[...], NN, HI).astype(bf16)
    lh[...] = left_h.reshape(lh.shape)
    ready()
    got_l = [send(lh.at[x, z], oth.at[x, z], s_l, 0, at.at(dg=1))]
    rt[...] = mm(left_h, bufh[...], TN).reshape(rt.shape)
    got_rt = [send(rt.at[wrap(r, d, nr)], rrt.at[d - 1], s_rt, d - 1, at.at(dr=d)) for d in range(1, nr)]
    tl[...] = mm(tok[...], left_h).reshape(tl.shape)
    got_tl = [send(tl.at[wrap(r, d, nr)], rtl.at[d - 1], s_tl, d - 1, at.at(dr=d)) for d in range(1, nr)]
    arrived(got_l)
    got_lz = [send(oth.at[x, z], oth.at[x, z], s_lz, d - 1, at.at(dz=d)) for d in range(1, nz)]

    arrived(got_rt)
    share = rt[r] + jnp.sum(rrt[...], axis=0)
    rt[r] = share
    rh[r] = share.astype(bf16)
    sho[...] = rt[r, :, pl.ds(pl.multiple_of(o * half, half), half)].astype(bf16)
    got_sh = [send(sho, rho.at[r], s_sh, 0, at.at(dg=1))]
    eye = lax.broadcasted_iota(jnp.int32, (kr, 128), 0) == lax.broadcasted_iota(jnp.int32, (kr, 128), 1)
    squares = jnp.sum(share * share, axis=1, keepdims=True)
    line = jnp.sum(jnp.where(eye, squares, 0.0), axis=0, keepdims=True)
    rsq[g, c] = line
    sq[...] = line
    got_sq = [send(sq, rsq.at[g, c], s_sq, k, at.at(dg=dg, dz=dz, dx=dx)) for k, (dg, dz, dx) in enumerate(column)]
    got_rh = [send(rh.at[r], rh.at[r], s_rh, d - 1, at.at(dr=d)) for d in range(1, nr)]
    arrived(got_lz)
    got_lx = [send(oth.at[x], oth.at[x], s_lx, d - 1, at.at(dx=d)) for d in range(1, nx)]
    arrived(got_sq)
    nb[r] = jnp.sum(rsq[...], axis=1)
    got_nb = [send(nb.at[r], nb.at[r], s_nb, d - 1, at.at(dr=d)) for d in range(1, nr)]
    arrived(got_sh)
    got_ro = [send(rho.at[r], rho.at[r], s_ro, d - 1, at.at(dr=d)) for d in range(1, nr)]
    arrived(got_tl)
    tls[...] = tl[r] + jnp.sum(rtl[...], axis=0)
    got_to = [send(tls, tlo, s_to, 0, at.at(dg=1))]
    fac_o[...] = (share.T / jnp.sqrt(nb[r, g][:, :kr] + EPSILON))
    arrived(got_rh)
    mom_o[...] = buffer - FEEDBACK * mm(left_h, rh[...].reshape(RANK, -1))

    arrived(got_nb)

    def normalised(p, right):
        norms = jnp.sqrt(nb[:, p] + EPSILON)
        norms = jnp.broadcast_to(norms, (nr, kr, 128))
        norms = jnp.sum(jnp.where(eye[None], norms, 0.0), axis=2, keepdims=True)
        return (right.astype(f32) / norms).astype(bf16).reshape(RANK, -1)

    own_q = normalised(g, rh[:, :, pl.ds(pl.multiple_of(g * half, half), half)])
    new_o[g] = w[g] - STEP * mm(left_h, own_q)
    own_pre = base[g] - STEP * mm(tls[...], own_q.astype(f32), NN, HI)
    arrived(got_ro)
    other_q = normalised(o, rho[...])
    arrived(got_lx)
    new_o[o] = w[o] - STEP * mm(oth[...].reshape(-1, RANK), other_q)
    arrived(got_to)
    other_pre = base[o] - STEP * mm(tlo[...], other_q.astype(f32), NN, HI)
    gate = jnp.where(g == 0, own_pre, other_pre)
    up = jnp.where(g == 0, other_pre, own_pre)
    hid_o[...] = (gate / (1.0 + jnp.exp(-gate)) * up).astype(bf16)
    for copies in (got_l, got_rt, got_tl, got_lz, got_sh, got_sq, got_rh, got_lx, got_nb, got_ro, got_to):
        for copy in copies:
            copy.wait_send()


def vmem(*shape, dtype=f32):
    return pltpu.VMEM(shape, dtype)


def pairs(n):
    return pltpu.SemaphoreType.DMA((2, n))


def call(kernel, outs, scratch, collective_id, *args):
    return pl.pallas_call(
        kernel,
        out_shape=[jax.ShapeDtypeStruct(s, t) for s, t in outs],
        in_specs=[pl.BlockSpec(memory_space=pltpu.VMEM)] * len(args),
        out_specs=[pl.BlockSpec(memory_space=pltpu.VMEM)] * len(outs),
        scratch_shapes=scratch,
        compiler_params=pltpu.CompilerParams(
            collective_id=collective_id, has_side_effects=True, vmem_limit_bytes=40 << 20
        ),
    )(*args)


def inverse_factor(gram):
    factor_l = jnp.linalg.cholesky(gram)
    return jax.scipy.linalg.solve_triangular(factor_l, jnp.eye(RANK, dtype=f32), lower=True).T


def local(sizes, momentum, gradient, factor_q, weights, tokens):
    nr, nc, ng = sizes
    nx, nz = NX, nc // NX
    mom, grad, fq = momentum[0], gradient[0], factor_q[0]
    rows, hid = mom.shape
    part, kr, nb = nx * nr, RANK // nr, BATCH // nr
    half = hid // ng
    left, gram, base = call(
        functools.partial(left_kernel, sizes),
        [((rows, RANK), f32), ((RANK, RANK), f32), ((2, nb, half), f32)],
        [
            vmem(rows, hid, dtype=bf16), vmem(nr, kr, hid, dtype=bf16),
            vmem(nx, rows // nx, RANK), vmem(nx - 1, rows // nx, RANK),
            vmem(nz, rows // nc, RANK), vmem(nz - 1, rows // nc, RANK), vmem(nx, nz, rows // nc, RANK),
            vmem(part, RANK // part, RANK), vmem(part - 1, RANK // part, RANK), vmem(part, RANK // part, RANK),
            vmem(nr, 2, nb, half), vmem(nr - 1, 2, nb, half),
            pairs(nr - 1), pairs(nx - 1), pairs(nz - 1), pairs(nz - 1), pairs(nx - 1), pairs(part - 1), pairs(part - 1),
            pairs(nr - 1),
        ],
        0, mom, grad, fq, weights, tokens,
    )
    wt = inverse_factor(gram)
    mom_new, fac, new, hidden = call(
        functools.partial(right_kernel, sizes),
        [((rows, hid), f32), ((hid, kr), f32), (weights.shape, f32), ((nb, half), bf16)],
        [
            vmem(rows, hid, dtype=bf16), vmem(nx, nz, rows // nc, RANK, dtype=bf16),
            vmem(nx, nz, rows // nc, RANK, dtype=bf16), vmem(nr, kr, hid), vmem(nr - 1, kr, hid),
            vmem(nr, nb, RANK), vmem(nr - 1, nb, RANK), vmem(nb, RANK), vmem(nb, RANK),
            vmem(nr, kr, hid, dtype=bf16), vmem(kr, half, dtype=bf16), vmem(nr, kr, half, dtype=bf16),
            vmem(1, 128), vmem(ng, nc, 1, 128), vmem(nr, ng, 1, 128),
            pairs(1), pairs(nr - 1), pairs(nr - 1), pairs(nz - 1), pairs(nx - 1), pairs(nr - 1), pairs(1), pairs(nr - 1),
            pairs(ng * nc - 1), pairs(nr - 1), pairs(1),
        ],
        1, mom, grad, left, wt, weights, base, tokens,
    )
    return mom_new[None], fac[None], new, hidden


def solution(mesh):
    sizes = tuple(mesh.shape[a] for a in ("row", "col", "grp"))
    in_specs = (
        P("grp", "row", "col"),
        P("grp", "row", "col"),
        P("grp", "col", "row"),
        P(None, "row", ("col", "grp")),
        P(None, "row"),
    )
    out_specs = (
        P("grp", "row", "col"),
        P("grp", "col", "row"),
        P(None, "row", ("col", "grp")),
        P("row", ("col", "grp")),
    )
    return jax.shard_map(
        functools.partial(local, sizes), mesh=mesh, in_specs=in_specs, out_specs=out_specs, check_vma=False
    )
```

time: 315 us -> 185 us (0.59)
  blocking collectives: 118 us -> 0 us
  Pallas kernels: 0 us -> 98.5 us
  waiting for transfers between devices: 65 us -> 0 us
  starting transfers between devices: 47.3 us -> 0 us
  local copies, waits for them, and re-layouts: 11 us -> 21.6 us
  other arithmetic: 60.4 us -> 57.1 us
    all_to_all x4 -> x0, blocking collectives: 102 us -> none  [the longest x2 52.4 us: sent_to_all(): return lax.all_to_all(copies, axis, split_axis=0, concat_axis=0, tiled=True)]
    pallas_call x0 -> x2, Pallas kernels: none -> 98.5 us  [call(): pl.pallas_call(kernel, out_shape=[jax.ShapeDtypeStruct(s, t) for s, t in...]
    all_to_all x5 -> x0, waiting for transfers between devices: 65 us -> none  [the longest x3 45.2 us: sent_to_all(): return lax.all_to_all(copies, axis, split_axis=0, concat_axis=0, tiled=True)]
    all_to_all x5 -> x0, starting transfers between devices: 47.3 us -> none  [the longest x3 21 us: sent_to_all(): return lax.all_to_all(copies, axis, split_axis=0, concat_axis=0, tiled=True)]
    all_gather x1 -> x0, blocking collectives: 15.4 us -> none  [rows_first(): whole = lax.all_gather(both, axis, axis=0, tiled=True)]
    unnamed x17 -> x29, local copies, waits for them, and re-layouts: 2.15 us -> 12.7 us
    dot_general x6 -> x0, matrix products: 5.91 us -> none  [the longest x1 2.42 us: local(): lax.dot_general(left_h, right_h, (((1,), (1,)), ((), ())), preferred_elem...]
    another operation x9 -> x10, local copies, waits for them, and re-layouts: 4.05 us -> 8.79 us
  transfers between devices with their start and end apart: 5 -> 0, of which waited for: 5 -> 0; matrix products, arithmetic and copies ran while one was open for 2% -> 0% of each run, Pallas kernels for 0% -> 0%
where the time goes in v1:
time: 185 us; the launch traced here: 184 us
  Pallas kernels  98.5 us (53%)
  other arithmetic  57.1 us (31%)
  local copies, waits for them, and re-layouts  21.6 us (12%)
  matrix products  4.61 us (2%)
  between operations  2.14 us (1%)
    pallas_call x2, Pallas kernels, call(): pl.pallas_call(kernel, out_shape=[jax.ShapeDtypeStruct(s, t) for s, t in...  98.5 us
    another operation x6, other arithmetic, inverse_factor(): factor_l = jnp.linalg.cholesky(gram)  34.1 us
    another operation x3, other arithmetic, inverse_factor(): jax.scipy.linalg.solve_triangular(factor_l, jnp.eye(RANK, dtype=f32), low...  21.9 us
    unnamed x29, local copies, waits for them, and re-layouts  12.7 us
    another operation x6, local copies, waits for them, and re-layouts  7.04 us
    another operation x3, matrix products, inverse_factor(): jax.scipy.linalg.solve_triangular(factor_l, jnp.eye(RANK, dtype=f32), low...  4.14 us

profile of v1, /device:TPU:1, one launch (start us, length us, event | category | flops | bytes accessed | tf_op | source)
XLA Modules:
  0.0 183.9 jit_solution(11222846069125543112)
XLA Ops:
  0.8 1.0 copy.9
  1.8 1.2 copy-done
  3.0 1.2 copy-done.2
  4.2 1.0 copy-done.4
  5.2 59.2 %shard_map.84 = (f32[512,256]{1,0:T(8,128)S(1)}, f32[256,256]{1,0:T(8,128)S(1)}, f32[2,32,256]{2,1,0:T(8,128)S(1)}) custom-call(f32[512,512]{1,0:T(8,128)S(1)} %bitcast.38, bf16[512,512]{1,0:T(8,128)(2,1)S(1)} %bitcast.40, f32[512,32]{1,0:T(8,128)S(1)} %bitcast.42, f32[2,512,256]{2,1,0:T(8,128)S(1)} %copy-done.2, bf16[256,512]{1,0:T(8,128)(2,1)S(1)} %copy-done.6), custom_call_target="tpu_custom_call" | custom-call | tf_op jit(solution)/shard_map/pallas_call | solution.py:205
  64.5 0.1 copy.10
  64.7 11.7 %cholesky.50 = f32[128,128]{1,0:T(8,128)S(1)} custom-call(f32[128,128]{1,0:T(8,128)S(1)} %cholesky.118), custom_call_target="Cholesky" | custom-call | tf_op jit(solution)/shard_map/jit(cholesky)/cholesky | solution.py:218
  76.4 9.8 %custom-call.15 = f32[1,128,128]{1,2,0:T(8,128)S(1)} custom-call(f32[1,128,128]{2,1,0:T(8,128)S(1)} %get-tuple-element.43), custom_call_target="InvertDiagBlocksLowerTriangular" | custom-call | tf_op jit(solution)/shard_map/jit(cholesky)/cholesky | solution.py:218
  86.3 0.2 constant_dynamic-update-slice_fusion.1
  86.5 0.3 convolution_subtract_fusion.1
  86.8 11.9 %cholesky.105 = f32[128,128]{1,0:T(8,128)S(1)} custom-call(f32[128,128]{1,0:T(8,128)S(1)} %convolution_subtract_fusion.1), custom_call_target="Cholesky" | custom-call | tf_op jit(solution)/shard_map/jit(cholesky)/cholesky | solution.py:218
  98.7 0.6 compare_reduce_fusion
  100.6 0.7 select_select_fusion
  101.4 7.0 %while.1 = (s32[]{:T(128)}, f32[256,256]{1,0:T(8,128)}, s32[2,2]{1,0:T(2,128)S(1)}, f32[2,128,128]{2,1,0:T(8,128)}, s32[]{:T(128)}) while((s32[]{:T(128)}, f32[256,256]{1,0:T(8,128)}, s32[2,2]{1,0:T(2,128)S(1)}, f32[2,128,128]{2,1,0:T(8,128)}, s32[]{:T(128)}) %tuple.28), condition=%wide.while_cond, body=%wide.while_body.sunk | while | flops 2 | bytes 132205 | solution.py:219
  101.4 0.6 fusion.14
  102.0 3.0 %bitcast_dynamic-update-slice_fusion.2 = f32[2,128,128]{2,1,0:T(8,128)} fusion(f32[2,128,128]{2,1,0:T(8,128)} %get-tuple-element.85, s32[]{:T(128)S(6)} %copy.20, f32[256,256]{1,0:T(8,128)} %get-tuple-element.88, s32[]{:T(128)} %bitcast.36, s32[]{:T(128)} %bitcast.37), kind=kLoop, calls=%fused_computation.clone.1 | loop fusion | bytes 132100 | tf_op jit(solution)/shard_map/jit(_solve_triangular)/triangular_solve
  104.9 0.6 fusion.14
  105.5 2.9 %bitcast_dynamic-update-slice_fusion.2 = f32[2,128,128]{2,1,0:T(8,128)} fusion(f32[2,128,128]{2,1,0:T(8,128)} %get-tuple-element.85, s32[]{:T(128)S(6)} %copy.20, f32[256,256]{1,0:T(8,128)} %get-tuple-element.88, s32[]{:T(128)} %bitcast.36, s32[]{:T(128)} %bitcast.37), kind=kLoop, calls=%fused_computation.clone.1 | loop fusion | bytes 132100 | tf_op jit(solution)/shard_map/jit(_solve_triangular)/triangular_solve
  108.4 21.2 %custom-call.16 = f32[2,128,128]{1,2,0:T(8,128)} custom-call(f32[2,128,128]{2,1,0:T(8,128)} %get-tuple-element.25), custom_call_target="InvertDiagBlocksLowerTriangular" | custom-call | tf_op jit(solution)/shard_map/jit(_solve_triangular)/triangular_solve | solution.py:219
  129.6 1.1 fusion.1
  130.7 1.1 convolution_subtract_fusion
  131.9 1.9 %fusion.4 = f32[128,256]{0,1:T(8,128)} fusion(f32[128,256]{1,0:T(8,128)S(1)} %convolution_subtract_fusion, f32[2,128,128]{1,2,0:T(8,128)} %custom-call.16), kind=kOutput, calls=%fused_computation.14 | convolution fusion | flops 50331648 | bytes 327680 | tf_op jit(solution)/shard_map/jit(_solve_triangular)/triangular_solve | solution.py:219
  133.8 1.7 copy.11
  135.4 1.0 maximum_bitcast_fusion.wt
  136.5 39.2 %shard_map.85 = (f32[512,512]{1,0:T(8,128)S(1)}, f32[512,32]{1,0:T(8,128)S(1)}, f32[2,512,256]{2,1,0:T(8,128)S(1)}, bf16[32,256]{1,0:T(8,128)(2,1)S(1)}) custom-call(f32[512,512]{1,0:T(8,128)S(1)} %bitcast.39, bf16[512,512]{1,0:T(8,128)(2,1)S(1)} %bitcast.41, f32[512,256]{1,0:T(8,128)S(1)} %get-tuple-element.11.left, f32[256,256]{1,0:T(8,128)S(1)} %maximum_bitcast_fusion.wt, ...), custom_call_target="tpu_custom_call" | custom-call | tf_op jit(solution)/shard_map/pallas_call | solution.py:205
  175.7 1.0 copy-done.7
  176.7 1.0 copy-done.9
  177.6 0.7 copy-done.10
  178.3 1.7 copy.13
  180.0 2.4 %copy.30 = f32[1,512,512]{2,1,0:T(8,128)} copy(f32[1,512,512]{2,1,0:T(8,128)} %bitcast.43) | data formatting | bytes 2097152
  182.4 1.0 copy.31
  183.3 0.6 copy.32
  (29 shorter events, 0.3 us)
Async XLA Ops:
  0.6 1.1 copy-start.6
  1.7 1.2 copy-start
  3.0 1.2 copy-start.2
  4.2 1.0 copy-start.4
  86.5 50.0 %copy-start.5 = (bf16[1,512,512]{2,1,0:T(8,128)(2,1)S(1)}, bf16[1,512,512]{2,1,0:T(8,128)(2,1)}, u32[]{:S(2)}) copy-start(bf16[1,512,512]{2,1,0:T(8,128)(2,1)} %param.6) | copy-start | bytes 1572868
  100.6 35.8 %copy-start.3 = (f32[2,512,256]{2,1,0:T(8,128)S(1)}, f32[2,512,256]{2,1,0:T(8,128)}, u32[]{:S(2)}) copy-start(f32[2,512,256]{2,1,0:T(8,128)} %w.3) | copy-start | bytes 3145732
  108.4 28.0 %copy-start.1 = (f32[1,512,512]{2,1,0:T(8,128)S(1)}, f32[1,512,512]{2,1,0:T(8,128)}, u32[]{:S(2)}) copy-start(f32[1,512,512]{2,1,0:T(8,128)} %param.5) | copy-start | bytes 3145732
  130.7 1.2 copy-start.11
  175.7 1.0 copy-start.7
  176.7 1.0 copy-start.9
  177.6 0.7 copy-start.10
  180.0 2.4 %copy-start.8 = (f32[2,512,256]{2,1,0:T(8,128)S(1)}, f32[2,512,256]{2,1,0:T(8,128)}, u32[]{:S(2)}) copy-start(f32[2,512,256]{2,1,0:T(8,128)} %copy-done.7) | copy-start | bytes 3145732

commit v2 on v1

v2 whole, which is shorter than its diff:
```python
import functools
import math

import jax
import jax.numpy as jnp
from jax import lax
from jax.experimental import pallas as pl
from jax.experimental.pallas import tpu as pltpu
from jax.sharding import PartitionSpec as P

D = 4096
HID = 16384
RANK = 256
BATCH = 256
FEEDBACK = 0.05
EPSILON = 1e-06
STEP = 0.4 * math.sqrt(max(D, HID))
CHUNKS = 4
NX = 4

f32, bf16 = jnp.float32, jnp.bfloat16
HI = lax.Precision.HIGHEST
MESH = pl.DeviceIdType.MESH
NN = (((1,), (0,)), ((), ()))
NT = (((1,), (1,)), ((), ()))
TN = (((0,), (0,)), ((), ()))


def mm(a, b, dims=NN, precision=None):
    return lax.dot_general(a, b, dims, precision=precision, preferred_element_type=f32)


def around(i, n):
    return [i if d == 0 else i + d - jnp.where(i + d >= n, n, 0) for d in range(n)]


class Place:
    def __init__(self, sizes):
        self.nr, self.nc, self.ng = sizes
        self.nx, self.nz = NX, self.nc // NX
        self.r, self.c, self.g = (lax.axis_index(a) for a in ("row", "col", "grp"))
        self.x, self.z = lax.rem(self.c, self.nx), lax.div(self.c, self.nx)
        self.rs, self.xs, self.zs = around(self.r, self.nr), around(self.x, self.nx), around(self.z, self.nz)
        self.gs = [self.g, 1 - self.g]

    def at(self, dr=0, dx=0, dz=0, dg=0):
        return (self.rs[dr], self.zs[dz] * self.nx + self.xs[dx], self.gs[dg])


def greet(partners):
    barrier = pltpu.get_barrier_semaphore()
    for device in partners:
        pl.semaphore_signal(barrier, inc=1, device_id=device, device_id_type=MESH)
    return lambda: pl.semaphore_wait(barrier, len(partners))


def send(src, dst, sems, k, device):
    copy = pltpu.make_async_remote_copy(
        src_ref=src, dst_ref=dst, send_sem=sems.at[0, k], recv_sem=sems.at[1, k], device_id=device, device_id_type=MESH
    )
    copy.start()
    return copy


def arrived(copies):
    for copy in copies:
        copy.wait_recv()


def left_kernel(sizes, mom_h, grad_h, fq_h, w_h, tok_h, left_o, gram_o, base_o, bufh,
                mom, grad, fq, w, tok, s_in, qbuf, part, partb, rx, sx, sxb, rz, l512, gp, rg, gf, pre, rpre,
                s_q, s_x, s_z, s_az, s_ax, s_g, s_ag, s_p):
    at = Place(sizes)
    nr, nx, nz = at.nr, at.nx, at.nz
    plane = [(dx, dr) for dx in range(nx) for dr in range(nr) if dx or dr]
    ready = greet([at.at(dr=dr, dx=dx) for dx, dr in plane] + [at.at(dz=d) for d in range(1, nz)])
    r, x, z = at.r, at.x, at.z
    loads = [
        pltpu.make_async_copy(a, b, s_in.at[k])
        for k, (a, b) in enumerate(((fq_h, fq), (mom_h, mom), (grad_h, grad), (tok_h, tok), (w_h, w)))
    ]
    for load in loads:
        load.start()
    loads[0].wait()
    qbuf[r] = fq[...].astype(bf16)
    ready()
    got_q = [send(qbuf.at[r], qbuf.at[r], s_q, d - 1, at.at(dr=d)) for d in range(1, nr)]
    loads[1].wait()
    loads[2].wait()
    bufh[...] = (mom[...] + grad[...].astype(f32)).astype(bf16)
    arrived(got_q)
    part[...] = mm(bufh[...], qbuf[...].reshape(RANK, -1), NT).reshape(part.shape)
    partb[...] = part[...].astype(bf16)
    got_x = [send(partb.at[at.xs[d]], rx.at[d - 1], s_x, d - 1, at.at(dx=d)) for d in range(1, nx)]
    loads[3].wait()
    loads[4].wait()
    for p in range(2):
        high = w[p].astype(bf16)
        low = (w[p] - high.astype(f32)).astype(bf16)
        pre[:, p] = (mm(tok[...], high) + mm(tok[...], low)).reshape(pre[:, p].shape)
    arrived(got_x)
    sx[...] = (part[x] + jnp.sum(rx[...].astype(f32), axis=0)).reshape(sx.shape)
    sxb[...] = sx[...].astype(bf16)
    got_z = [send(sxb.at[at.zs[d]], rz.at[d - 1], s_z, d - 1, at.at(dz=d)) for d in range(1, nz)]
    got_p = [send(pre.at[at.rs[d]], rpre.at[d - 1], s_p, d - 1, at.at(dr=d)) for d in range(1, nr)]
    arrived(got_z)
    l512[x, z] = (sx[z] + jnp.sum(rz[...].astype(f32), axis=0)).astype(bf16)
    got_az = [send(l512.at[x, z], l512.at[x, z], s_az, d - 1, at.at(dz=d)) for d in range(1, nz)]
    arrived(got_az)
    rows = l512[x].reshape(-1, RANK)
    gp[...] = mm(rows, rows, TN).reshape(gp.shape)
    got_g = []
    for k, (dx, dr) in enumerate(plane):
        m = at.xs[dx] * nr + at.rs[dr]
        got_g.append(send(gp.at[m], rg.at[k], s_g, k, at.at(dr=dr, dx=dx)))
    got_ax = [send(l512.at[x], l512.at[x], s_ax, d - 1, at.at(dx=d)) for d in range(1, nx)]
    arrived(got_g)
    m = x * nr + r
    gf[m] = gp[m] + jnp.sum(rg[...], axis=0)
    got_ag = [send(gf.at[m], gf.at[m], s_ag, k, at.at(dr=dr, dx=dx)) for k, (dx, dr) in enumerate(plane)]
    arrived(got_p)
    base_o[...] = pre[r] + jnp.sum(rpre[...], axis=0)
    arrived(got_ax)
    left_o[...] = l512[...].reshape(left_o.shape)
    arrived(got_ag)
    gram_o[...] = gf[...].reshape(gram_o.shape)
    for copies in (got_q, got_x, got_p, got_z, got_az, got_g, got_ax, got_ag):
        for copy in copies:
            copy.wait_send()


def right_kernel(sizes, bufh, left, linv, tok, lh_o, oth_o, rh_o, rho_o, nb_o, share_o, tl_o,
                 lh, oth, rt, rtb, rrt, tl, tlb, rtl, tls, tlo, rh, sho, rho, sq, sqx, sqz, nb,
                 s_l, s_rt, s_tl, s_lz, s_lx, s_rh, s_sh, s_ro, s_sq, s_sz, s_nb, s_to):
    at = Place(sizes)
    nr, nx, nz, ng = at.nr, at.nx, at.nz, at.ng
    r, c, g, x, z = at.r, at.c, at.g, at.x, at.z
    side = [(dx, dg) for dx in range(nx) for dg in range(ng) if dx or dg]
    ready = greet(
        [at.at(dr=d) for d in range(1, nr)] + [at.at(dz=d) for d in range(1, nz)] + [at.at(dx=dx, dg=dg) for dx, dg in side]
    )
    o = 1 - g
    kr = RANK // nr
    half = sho.shape[1]

    high = linv[...].astype(bf16)
    low = (linv[...] - high.astype(f32)).astype(bf16)
    left_h = (mm(left[...], high, NT) + mm(left[...], low, NT)).astype(bf16)
    lh[...] = left_h.reshape(lh.shape)
    ready()
    got_l = [send(lh.at[x, z], oth.at[x, z], s_l, 0, at.at(dg=1))]
    rt[...] = mm(left_h, bufh[...], TN).reshape(rt.shape)
    rtb[...] = rt[...].astype(bf16)
    got_rt = [send(rtb.at[at.rs[d]], rrt.at[d - 1], s_rt, d - 1, at.at(dr=d)) for d in range(1, nr)]
    tl[...] = mm(tok[...], left_h).reshape(tl.shape)
    tlb[...] = tl[...].astype(bf16)
    got_tl = [send(tlb.at[at.rs[d]], rtl.at[d - 1], s_tl, d - 1, at.at(dr=d)) for d in range(1, nr)]
    arrived(got_rt)
    share = rt[r] + jnp.sum(rrt[...].astype(f32), axis=0)
    share_o[...] = share
    rh[r] = share.astype(bf16)
    sho[...] = share_o[:, pl.ds(pl.multiple_of(o * half, half), half)].astype(bf16)
    got_sh = [send(sho, rho.at[r], s_sh, 0, at.at(dg=1))]
    eye = lax.broadcasted_iota(jnp.int32, (kr, 128), 0) == lax.broadcasted_iota(jnp.int32, (kr, 128), 1)
    squares = jnp.sum(share * share, axis=1, keepdims=True)
    line = jnp.sum(jnp.where(eye, squares, 0.0), axis=0, keepdims=True)
    sqx[g, x] = line
    sq[...] = line
    got_sq = [send(sq, sqx.at[g, x], s_sq, k, at.at(dx=dx, dg=dg)) for k, (dx, dg) in enumerate(side)]
    got_rh = [send(rh.at[r], rh.at[r], s_rh, d - 1, at.at(dr=d)) for d in range(1, nr)]
    arrived(got_l)
    got_lz = [send(oth.at[x, z], oth.at[x, z], s_lz, d - 1, at.at(dz=d)) for d in range(1, nz)]
    arrived(got_sq)
    sqz[z] = jnp.sum(sqx[...], axis=1)
    got_sz = [send(sqz.at[z], sqz.at[z], s_sz, d - 1, at.at(dz=d)) for d in range(1, nz)]
    arrived(got_sh)
    got_ro = [send(rho.at[r], rho.at[r], s_ro, d - 1, at.at(dr=d)) for d in range(1, nr)]
    arrived(got_sz)
    nb[r] = jnp.sum(sqz[...], axis=0)
    got_nb = [send(nb.at[r], nb.at[r], s_nb, d - 1, at.at(dr=d)) for d in range(1, nr)]
    arrived(got_lz)
    got_lx = [send(oth.at[x], oth.at[x], s_lx, d - 1, at.at(dx=d)) for d in range(1, nx)]
    arrived(got_tl)
    tls[...] = (tl[r] + jnp.sum(rtl[...].astype(f32), axis=0)).astype(bf16)
    got_to = [send(tls, tlo, s_to, 0, at.at(dg=1))]
    lh_o[...] = lh[...].reshape(lh_o.shape)
    arrived(got_rh)
    rh_o[...] = rh[...].reshape(rh_o.shape)
    arrived(got_lx)
    oth_o[...] = oth[...].reshape(oth_o.shape)
    arrived(got_nb)
    nb_o[...] = nb[...]
    arrived(got_ro)
    rho_o[...] = rho[...]
    arrived(got_to)
    tl_o[0] = tls[...]
    tl_o[1] = tlo[...]
    for copies in (got_l, got_rt, got_tl, got_lz, got_sh, got_sq, got_sz, got_rh, got_lx, got_nb, got_ro, got_to):
        for copy in copies:
            copy.wait_send()


def last_kernel(mom, grad, w, base, lh, oth, rh, rho, nb, share, tl, mom_h, new_h, fac_o, hid_o, mom_v, new_v, sems):
    r, g = lax.axis_index("row"), lax.axis_index("grp")
    o = 1 - g
    nr, kr, half = rho.shape
    rows = lh.shape[0]
    chunk = rows // CHUNKS
    copies = []

    def out(src, dst):
        copies.append(pltpu.make_async_copy(src, dst, sems.at[len(copies)]))
        copies[-1].start()

    for k in range(CHUNKS):
        at = pl.ds(k * chunk, chunk)
        mom_v[at] = mom[at] + grad[at].astype(f32) - FEEDBACK * mm(lh[at], rh[...])
        out(mom_v.at[at], mom_h.at[at])
    eye = lax.broadcasted_iota(jnp.int32, (kr, 128), 0) == lax.broadcasted_iota(jnp.int32, (kr, 128), 1)

    def columns(norms):
        norms = jnp.broadcast_to(jnp.sqrt(norms + EPSILON), (norms.shape[0], kr, 128))
        return jnp.sum(jnp.where(eye[None], norms, 0.0), axis=2, keepdims=True)

    own = rh[:, pl.ds(pl.multiple_of(g * half, half), half)].astype(f32).reshape(rho.shape)
    own_q = (own / columns(nb[:, g])).astype(bf16).reshape(RANK, half)
    other_q = (rho[...].astype(f32) / columns(nb[:, o])).astype(bf16).reshape(RANK, half)
    for p, q, factor in ((g, own_q, lh), (o, other_q, oth)):
        for k in range(CHUNKS):
            at = pl.ds(k * chunk, chunk)
            new_v[p, at] = w[p, at] - STEP * mm(factor[at], q)
            out(new_v.at[p, at], new_h.at[p, at])
    fac_o[...] = share[...] / columns(nb[r, g][None])[0]
    own_pre = base[g] - STEP * mm(tl[0], own_q)
    other_pre = base[o] - STEP * mm(tl[1], other_q)
    gate = jnp.where(g == 0, own_pre, other_pre)
    up = jnp.where(g == 0, other_pre, own_pre)
    hid_o[...] = (gate / (1.0 + jnp.exp(-gate)) * up).astype(bf16)
    for copy in copies:
        copy.wait()


def tri_half(e):
    i, j = (lax.broadcasted_iota(jnp.int32, e.shape, d) for d in (0, 1))
    return jnp.where(i > j, e, jnp.where(i == j, 0.5 * e, 0.0))


def inverse_kernel(gram, inv_o, a, w, s):
    n = RANK
    i, j = (lax.broadcasted_iota(jnp.int32, (n, n), d) for d in (0, 1))
    eye = jnp.where(i == j, 1.0, 0.0)
    diagonal = jnp.where(i == j, gram[...], 0.0)
    down = lax.rsqrt(jnp.sum(diagonal, axis=1, keepdims=True))
    across = lax.rsqrt(jnp.sum(diagonal, axis=0, keepdims=True))
    a[...] = gram[...] * down * across
    first = jnp.where(i == j, 0.0, a[...])
    w[...] = eye - tri_half(first)

    def step(state):
        count, _ = state
        left = w[...]
        e = mm(mm(left, a[...], NN, HI), left, NT, HI) - eye
        w[...] = left - mm(tri_half(e), left, NN, HI)
        return count + 1, jnp.max(jnp.abs(e))

    _, worst = lax.while_loop(lambda t: (t[0] < 12) & ~(t[1] < 4e-4), step, (0, jnp.float32(1.0)))
    inv_o[...] = w[...] * across

    @pl.when(~(worst < 4e-4))
    def _():
        s[:, :n] = gram[...]
        s[:, n:] = eye
        row = lax.broadcasted_iota(jnp.int32, (n, 1), 0)

        def eliminate(k, _):
            line = s[pl.ds(k, 1), :]
            column = jnp.sum(jnp.where(j == k, s[:, :n], 0.0), axis=1, keepdims=True)
            pivot = jnp.sum(jnp.where(row == k, column, 0.0), axis=0, keepdims=True)
            s[...] = s[...] - jnp.where(row > k, column / pivot, 0.0) * line
            return 0

        lax.fori_loop(0, n, eliminate, 0)
        pivots = jnp.sum(jnp.where(i == j, s[:, :n], 0.0), axis=1, keepdims=True)
        inv_o[...] = s[:, n:] / jnp.sqrt(pivots)


def vmem(*shape, dtype=f32):
    return pltpu.VMEM(shape, dtype)


def pairs(n):
    return pltpu.SemaphoreType.DMA((2, n))


def call(kernel, ins, outs, scratch, args, collective_id=None, limit=24):
    where = {"v": pltpu.VMEM, "h": pltpu.HBM}
    params = {} if collective_id is None else dict(collective_id=collective_id, has_side_effects=True)
    return pl.pallas_call(
        kernel,
        out_shape=[jax.ShapeDtypeStruct(s, t) for s, t, _ in outs],
        in_specs=[pl.BlockSpec(memory_space=where[k]) for k in ins],
        out_specs=[pl.BlockSpec(memory_space=where[k]) for _, _, k in outs],
        scratch_shapes=scratch,
        compiler_params=pltpu.CompilerParams(vmem_limit_bytes=int(limit * 2**20), **params),
    )(*args)


def local(sizes, momentum, gradient, factor_q, weights, tokens):
    nr, nc, ng = sizes
    nx, nz = NX, nc // NX
    mom, grad, fq = momentum[0], gradient[0], factor_q[0].T
    rows, hid = mom.shape
    part, kr, nb = nx * nr, RANK // nr, BATCH // nr
    half = hid // ng
    left, gram, base, bufh = call(
        functools.partial(left_kernel, sizes),
        "hhhhh",
        [((rows, RANK), bf16, "v"), ((RANK, RANK), f32, "v"), ((2, nb, half), f32, "v"), ((rows, hid), bf16, "v")],
        [
            vmem(rows, hid), vmem(rows, hid, dtype=bf16), vmem(kr, hid), vmem(*weights.shape), vmem(*tokens.shape, dtype=bf16),
            pltpu.SemaphoreType.DMA((5,)), vmem(nr, kr, hid, dtype=bf16),
            vmem(nx, rows // nx, RANK), vmem(nx, rows // nx, RANK, dtype=bf16), vmem(nx - 1, rows // nx, RANK, dtype=bf16),
            vmem(nz, rows // nc, RANK), vmem(nz, rows // nc, RANK, dtype=bf16), vmem(nz - 1, rows // nc, RANK, dtype=bf16),
            vmem(nx, nz, rows // nc, RANK, dtype=bf16),
            vmem(part, RANK // part, RANK), vmem(part - 1, RANK // part, RANK), vmem(part, RANK // part, RANK),
            vmem(nr, 2, nb, half), vmem(nr - 1, 2, nb, half),
            pairs(nr - 1), pairs(nx - 1), pairs(nz - 1), pairs(nz - 1), pairs(nx - 1), pairs(part - 1), pairs(part - 1),
            pairs(nr - 1),
        ],
        (mom, grad, fq, weights, tokens), 0, limit=52.3,
    )
    (linv,) = call(
        inverse_kernel, "v", [((RANK, RANK), f32, "v")],
        [vmem(RANK, RANK), vmem(RANK, RANK), vmem(RANK, 2 * RANK)], (gram,),
    )
    lh, oth, rh, rho, norms, share, tl = call(
        functools.partial(right_kernel, sizes),
        "vvvv",
        [
            ((rows, RANK), bf16, "v"), ((rows, RANK), bf16, "v"), ((RANK, hid), bf16, "v"), ((nr, kr, half), bf16, "v"),
            ((nr, ng, 1, 128), f32, "v"), ((kr, hid), f32, "v"), ((2, nb, RANK), bf16, "v"),
        ],
        [
            vmem(nx, nz, rows // nc, RANK, dtype=bf16),
            vmem(nx, nz, rows // nc, RANK, dtype=bf16), vmem(nr, kr, hid), vmem(nr, kr, hid, dtype=bf16),
            vmem(nr - 1, kr, hid, dtype=bf16), vmem(nr, nb, RANK), vmem(nr, nb, RANK, dtype=bf16),
            vmem(nr - 1, nb, RANK, dtype=bf16), vmem(nb, RANK, dtype=bf16), vmem(nb, RANK, dtype=bf16),
            vmem(nr, kr, hid, dtype=bf16), vmem(kr, half, dtype=bf16), vmem(nr, kr, half, dtype=bf16),
            vmem(1, 128), vmem(ng, nx, 1, 128), vmem(nz, ng, 1, 128), vmem(nr, ng, 1, 128),
            pairs(1), pairs(nr - 1), pairs(nr - 1), pairs(nz - 1), pairs(nx - 1), pairs(nr - 1), pairs(1), pairs(nr - 1),
            pairs(ng * nx - 1), pairs(nz - 1), pairs(nr - 1), pairs(1),
        ],
        (bufh, left, linv, tokens), 1,
    )
    mom_new, new, fac, hidden = call(
        last_kernel, "v" * 11,
        [((rows, hid), f32, "h"), (weights.shape, f32, "h"), ((kr, hid), f32, "v"), ((nb, half), bf16, "v")],
        [vmem(rows, hid), vmem(*weights.shape), pltpu.SemaphoreType.DMA((3 * CHUNKS,))],
        (mom, grad, weights, base, lh, oth, rh, rho, norms, share, tl),
    )
    return mom_new[None], fac.T[None], new, hidden


def solution(mesh):
    sizes = tuple(mesh.shape[a] for a in ("row", "col", "grp"))
    in_specs = (
        P("grp", "row", "col"),
        P("grp", "row", "col"),
        P("grp", "col", "row"),
        P(None, "row", ("col", "grp")),
        P(None, "row"),
    )
    out_specs = (
        P("grp", "row", "col"),
        P("grp", "col", "row"),
        P(None, "row", ("col", "grp")),
        P("row", ("col", "grp")),
    )
    return jax.shard_map(
        functools.partial(local, sizes), mesh=mesh, in_specs=in_specs, out_specs=out_specs, check_vma=False
    )
```

time: 185 us -> 167 us (0.903)
  Pallas kernels: 98.5 us -> 164 us
  other arithmetic: 57.1 us -> 0 us
  local copies, waits for them, and re-layouts: 21.6 us -> 1.8 us
  matrix products: 4.61 us -> 0 us
    pallas_call x2 -> x4, Pallas kernels: 98.5 us -> 164 us  [call(): pl.pallas_call(kernel, out_shape=[jax.ShapeDtypeStruct(s, t) for s, t, _...]
    another operation x9 -> x0, other arithmetic: 56.1 us -> none  [the longest x6 34.1 us: inverse_factor(): factor_l = jnp.linalg.cholesky(gram)]
    unnamed x29 -> x10, local copies, waits for them, and re-layouts: 12.7 us -> 1.8 us
    another operation x10 -> x0, local copies, waits for them, and re-layouts: 8.79 us -> none
    another operation x5 -> x0, matrix products: 4.61 us -> none  [the longest x3 4.14 us: inverse_factor(): jax.scipy.linalg.solve_triangular(factor_l, jnp.eye(RANK, dtype=f32), low...]
where the time goes in v2:
time: 167 us
  Pallas kernels  164 us (98%)
  local copies, waits for them, and re-layouts  1.8 us (1%)
    pallas_call x4, Pallas kernels, call(): pl.pallas_call(kernel, out_shape=[jax.ShapeDtypeStruct(s, t) for s, t, _...  164 us

profile of v2, /device:TPU:1, one launch (start us, length us, event | category | flops | bytes accessed | tf_op | source)
XLA Modules:
  0.0 166.8 jit_solution(7961321255011188753)
XLA Ops:
  0.6 0.0 copy-start.3
  0.6 0.9 copy-done.3
  1.6 0.0 copy-start.4
  1.6 0.8 copy-done.4
  2.4 0.0 copy-start.1
  2.4 53.9 %shard_map.84 = (bf16[512,256]{1,0:T(8,128)(2,1)S(1)}, f32[256,256]{1,0:T(8,128)S(1)}, f32[2,32,256]{2,1,0:T(8,128)S(1)}, bf16[512,512]{1,0:T(8,128)(2,1)S(1)}) custom-call(f32[512,512]{1,0:T(8,128)} %bitcast.9, bf16[512,512]{1,0:T(8,128)(2,1)} %bitcast.11, f32[32,512]{1,0:T(8,128)S(1)} %bitcast.13, f32[2,512,256]{2,1,0:T(8,128)} %w.1, ...), custom_call_target="tpu_custom_call" | custom-call | tf_op jit(solution)/shard_map/pallas_call | solution.py:298
  56.4 0.0 copy-start
  56.4 71.6 %shard_map.85.linv = f32[256,256]{1,0:T(8,128)S(1)} custom-call(f32[256,256]{1,0:T(8,128)S(1)} %get-tuple-element.22.gram), custom_call_target="tpu_custom_call" | custom-call | tf_op jit(solution)/shard_map/pallas_call | solution.py:298
  128.0 0.0 copy-start.2
  128.0 36.5 %shard_map.86 = (bf16[512,256]{1,0:T(8,128)(2,1)S(1)}, bf16[512,256]{1,0:T(8,128)(2,1)S(1)}, bf16[256,512]{1,0:T(8,128)(2,1)S(1)}, bf16[8,32,256]{2,1,0:T(8,128)...) custom-call(bf16[512,512]{1,0:T(8,128)(2,1)S(1)} %get-tuple-element.20.bufh, ...), custom_call_target="tpu_custom_call" | custom-call | tf_op jit(solution)/shard_map/pallas_call | solution.py:298
  164.5 0.0 copy-done.1
  164.5 0.0 copy-done
  164.5 0.0 copy-done.2
  164.5 2.3 %shard_map.87 = (f32[512,512]{1,0:T(8,128)}, f32[2,512,256]{2,1,0:T(8,128)}, f32[32,512]{1,0:T(8,128)}, bf16[32,256]{1,0:T(8,128)(2,1)}) custom-call(f32[512,512]{1,0:T(8,128)S(1)} %bitcast.10, bf16[512,512]{1,0:T(8,128)(2,1)S(1)} %bitcast.12, f32[2,512,256]{2,1,0:T(8,128)S(1)} %copy-done.1, f32[2,32,256]{2,1,0:T(8,128)S(1)} %get-tuple-element.19.base, ...), custom_call_target="tpu_custom_call" | custom-call | tf_op jit(solution)/shard_map/pallas_call | solution.py:298
Async XLA Ops:
  0.6 1.0 copy-start.3
  1.6 0.8 copy-start.4
  2.4 162.1 %copy-start.1 = (f32[2,512,256]{2,1,0:T(8,128)S(1)}, f32[2,512,256]{2,1,0:T(8,128)}, u32[]{:S(2)}) copy-start(f32[2,512,256]{2,1,0:T(8,128)} %w.1) | copy-start | bytes 3145732
  56.4 108.2 %copy-start = (f32[1,512,512]{2,1,0:T(8,128)S(1)}, f32[1,512,512]{2,1,0:T(8,128)}, u32[]{:S(2)}) copy-start(f32[1,512,512]{2,1,0:T(8,128)} %param.5) | copy-start | bytes 3145732
  128.0 36.5 %copy-start.2 = (bf16[1,512,512]{2,1,0:T(8,128)(2,1)S(1)}, bf16[1,512,512]{2,1,0:T(8,128)(2,1)}, u32[]{:S(2)}) copy-start(bf16[1,512,512]{2,1,0:T(8,128)(2,1)} %param.6) | copy-start | bytes 1572868

commit v3 on v2

--- a/solution.py
+++ b/solution.py
@@ -16,6 +16,7 @@
 EPSILON = 1e-06
 STEP = 0.4 * math.sqrt(max(D, HID))
 CHUNKS = 4
+NEAR = 0.16
 NX = 4
 
 f32, bf16 = jnp.float32, jnp.bfloat16
@@ -108,7 +109,15 @@
     got_az = [send(l512.at[x, z], l512.at[x, z], s_az, d - 1, at.at(dz=d)) for d in range(1, nz)]
     arrived(got_az)
     rows = l512[x].reshape(-1, RANK)
-    gp[...] = mm(rows, rows, TN).reshape(gp.shape)
+    gram = mm(rows, rows, TN)
+    h = RANK // 2
+    i, j = (lax.broadcasted_iota(jnp.int32, (h, h), d) for d in (0, 1))
+    packed = jnp.where(i >= j, gram[:h, :h], gram[h:, h:])
+    gp[: gp.shape[0] // 2, :-1] = packed.reshape(gp.shape[0] // 2, -1, h)
+    gp[gp.shape[0] // 2 :, :-1] = gram[h:, :h].reshape(gp.shape[0] // 2, -1, h)
+    gp[:, -1:] = jnp.broadcast_to(
+        jnp.sum(jnp.where(i == j, gram[h:, h:], 0.0), axis=0, keepdims=True), (gp.shape[0], 1, h)
+    )
     got_g = []
     for k, (dx, dr) in enumerate(plane):
         m = at.xs[dx] * nr + at.rs[dr]
@@ -123,28 +132,87 @@
     arrived(got_ax)
     left_o[...] = l512[...].reshape(left_o.shape)
     arrived(got_ag)
-    gram_o[...] = gf[...].reshape(gram_o.shape)
+    gram_o[:RANK] = gf[:, :-1].reshape(RANK, -1)
+    gram_o[RANK:] = jnp.broadcast_to(gf[0, -1:], (8, gf.shape[2]))
     for copies in (got_q, got_x, got_p, got_z, got_az, got_g, got_ax, got_ag):
         for copy in copies:
             copy.wait_send()
 
 
-def right_kernel(sizes, bufh, left, linv, tok, lh_o, oth_o, rh_o, rho_o, nb_o, share_o, tl_o,
-                 lh, oth, rt, rtb, rrt, tl, tlb, rtl, tls, tlo, rh, sho, rho, sq, sqx, sqz, nb,
-                 s_l, s_rt, s_tl, s_lz, s_lx, s_rh, s_sh, s_ro, s_sq, s_sz, s_nb, s_to):
+def tri_half(e):
+    i, j = (lax.broadcasted_iota(jnp.int32, e.shape, d) for d in (0, 1))
+    return jnp.where(i > j, e, jnp.where(i == j, 0.5 * e, 0.0))
+
+
+def residual(w, a, precision=None):
+    i, j = (lax.broadcasted_iota(jnp.int32, a.shape, d) for d in (0, 1))
+    return mm(mm(w, a, NN, precision), w, NT, precision) - jnp.where(i == j, 1.0, 0.0)
+
+
+def start_kernel(packed, a_o, w_o, across_o, near_o, gram, s):
+    n, h = RANK, RANK // 2
+    i, j = (lax.broadcasted_iota(jnp.int32, (h, h), d) for d in (0, 1))
+    both, turned = packed[:h], packed[:h].T
+    gram[:h, :h] = jnp.where(i >= j, both, turned)
+    gram[h:, h:] = jnp.where(i > j, turned, jnp.where(i == j, packed[n : n + 1], both))
+    gram[h:, :h] = packed[h:n]
+    gram[:h, h:] = packed[h:n].T
+    i, j = (lax.broadcasted_iota(jnp.int32, (n, n), d) for d in (0, 1))
+    eye = jnp.where(i == j, 1.0, 0.0)
+    diagonal = jnp.where(i == j, gram[...], 0.0)
+    down = lax.rsqrt(jnp.sum(diagonal, axis=1, keepdims=True))
+    across = lax.rsqrt(jnp.sum(diagonal, axis=0, keepdims=True))
+    a = gram[...] * down * across
+    a_o[...] = a
+    across_o[...] = jnp.broadcast_to(across, across_o.shape)
+    w = eye - tri_half(jnp.where(i == j, 0.0, a))
+    w = w - mm(tri_half(residual(w, a)), w)
+    w_o[...] = w
+    e = residual(w, a)
+    far = jnp.sum(e * e)
+    near_o[...] = jnp.ones(near_o.shape, f32)
+
+    @pl.when(~(far < NEAR))
+    def _():
+        s[:, :n] = gram[...]
+        s[:, n:] = eye
+        row = lax.broadcasted_iota(jnp.int32, (n, 1), 0)
+
+        def eliminate(k, _):
+            line = s[pl.ds(k, 1), :]
+            column = jnp.sum(jnp.where(j == k, s[:, :n], 0.0), axis=1, keepdims=True)
+            pivot = jnp.sum(jnp.where(row == k, column, 0.0), axis=0, keepdims=True)
+            s[...] = s[...] - jnp.where(row > k, column / pivot, 0.0) * line
+            return 0
+
+        lax.fori_loop(0, n, eliminate, 0)
+        pivots = jnp.sum(jnp.where(i == j, s[:, :n], 0.0), axis=1, keepdims=True)
+        w_o[...] = s[:, n:] / jnp.sqrt(pivots)
+        across_o[...] = jnp.ones(across_o.shape, f32)
+        near_o[...] = jnp.zeros(near_o.shape, f32)
+
+
+def right_kernel(sizes, bufh, left, a, w, across, near, tok, lh_o, oth_o, rh_o, rho_o, nb_o, share_o, tl_o,
+                 lh, oth, rt, rtb, rrt, tl, tlb, rtl, tls, tlo, rh, sho, rho, sq, sqz, sqx, nb,
+                 s_l, s_rt, s_tl, s_lz, s_lx, s_rh, s_sh, s_ro, s_sq, s_sx, s_nb, s_to):
     at = Place(sizes)
     nr, nx, nz, ng = at.nr, at.nx, at.nz, at.ng
     r, c, g, x, z = at.r, at.c, at.g, at.x, at.z
-    side = [(dx, dg) for dx in range(nx) for dg in range(ng) if dx or dg]
+    line_up = [(dz, dg) for dz in range(nz) for dg in range(ng) if dz or dg]
     ready = greet(
-        [at.at(dr=d) for d in range(1, nr)] + [at.at(dz=d) for d in range(1, nz)] + [at.at(dx=dx, dg=dg) for dx, dg in side]
+        [at.at(dr=d) for d in range(1, nr)] + [at.at(dx=d) for d in range(1, nx)] + [at.at(dz=dz, dg=dg) for dz, dg in line_up]
     )
     o = 1 - g
     kr = RANK // nr
     half = sho.shape[1]
 
-    high = linv[...].astype(bf16)
-    low = (linv[...] - high.astype(f32)).astype(bf16)
+    inverse = w[...]
+    for _ in range(3):
+        error = jnp.where(near[:1, :1] > 0, tri_half(residual(inverse, a[...], HI)), 0.0)
+        inverse = inverse - mm(error, inverse, NN, HI)
+    inverse = inverse * across[:1]
+    high = inverse.astype(bf16)
+    low = (inverse - high.astype(f32)).astype(bf16)
     left_h = (mm(left[...], high, NT) + mm(left[...], low, NT)).astype(bf16)
     lh[...] = left_h.reshape(lh.shape)
     ready()
@@ -164,25 +232,25 @@
     eye = lax.broadcasted_iota(jnp.int32, (kr, 128), 0) == lax.broadcasted_iota(jnp.int32, (kr, 128), 1)
     squares = jnp.sum(share * share, axis=1, keepdims=True)
     line = jnp.sum(jnp.where(eye, squares, 0.0), axis=0, keepdims=True)
-    sqx[g, x] = line
+    sqz[g, z] = line
     sq[...] = line
-    got_sq = [send(sq, sqx.at[g, x], s_sq, k, at.at(dx=dx, dg=dg)) for k, (dx, dg) in enumerate(side)]
+    got_sq = [send(sq, sqz.at[g, z], s_sq, k, at.at(dz=dz, dg=dg)) for k, (dz, dg) in enumerate(line_up)]
     got_rh = [send(rh.at[r], rh.at[r], s_rh, d - 1, at.at(dr=d)) for d in range(1, nr)]
-    arrived(got_l)
-    got_lz = [send(oth.at[x, z], oth.at[x, z], s_lz, d - 1, at.at(dz=d)) for d in range(1, nz)]
-    arrived(got_sq)
-    sqz[z] = jnp.sum(sqx[...], axis=1)
-    got_sz = [send(sqz.at[z], sqz.at[z], s_sz, d - 1, at.at(dz=d)) for d in range(1, nz)]
-    arrived(got_sh)
-    got_ro = [send(rho.at[r], rho.at[r], s_ro, d - 1, at.at(dr=d)) for d in range(1, nr)]
-    arrived(got_sz)
-    nb[r] = jnp.sum(sqz[...], axis=0)
-    got_nb = [send(nb.at[r], nb.at[r], s_nb, d - 1, at.at(dr=d)) for d in range(1, nr)]
-    arrived(got_lz)
-    got_lx = [send(oth.at[x], oth.at[x], s_lx, d - 1, at.at(dx=d)) for d in range(1, nx)]
     arrived(got_tl)
     tls[...] = (tl[r] + jnp.sum(rtl[...].astype(f32), axis=0)).astype(bf16)
     got_to = [send(tls, tlo, s_to, 0, at.at(dg=1))]
+    arrived(got_l)
+    got_lz = [send(oth.at[x, z], oth.at[x, z], s_lz, d - 1, at.at(dz=d)) for d in range(1, nz)]
+    arrived(got_sh)
+    got_ro = [send(rho.at[r], rho.at[r], s_ro, d - 1, at.at(dr=d)) for d in range(1, nr)]
+    arrived(got_sq)
+    sqx[x] = jnp.sum(sqz[...], axis=1)
+    got_sx = [send(sqx.at[x], sqx.at[x], s_sx, d - 1, at.at(dx=d)) for d in range(1, nx)]
+    arrived(got_lz)
+    got_lx = [send(oth.at[x], oth.at[x], s_lx, d - 1, at.at(dx=d)) for d in range(1, nx)]
+    arrived(got_sx)
+    nb[r] = jnp.sum(sqx[...], axis=0)
+    got_nb = [send(nb.at[r], nb.at[r], s_nb, d - 1, at.at(dr=d)) for d in range(1, nr)]
     lh_o[...] = lh[...].reshape(lh_o.shape)
     arrived(got_rh)
     rh_o[...] = rh[...].reshape(rh_o.shape)
@@ -195,7 +263,7 @@
     arrived(got_to)
     tl_o[0] = tls[...]
     tl_o[1] = tlo[...]
-    for copies in (got_l, got_rt, got_tl, got_lz, got_sh, got_sq, got_sz, got_rh, got_lx, got_nb, got_ro, got_to):
+    for copies in (got_l, got_rt, got_tl, got_lz, got_sh, got_sq, got_sx, got_rh, got_lx, got_nb, got_ro, got_to):
         for copy in copies:
             copy.wait_send()
 
@@ -240,50 +308,6 @@
         copy.wait()
 
 
-def tri_half(e):
-    i, j = (lax.broadcasted_iota(jnp.int32, e.shape, d) for d in (0, 1))
-    return jnp.where(i > j, e, jnp.where(i == j, 0.5 * e, 0.0))
-
-
-def inverse_kernel(gram, inv_o, a, w, s):
-    n = RANK
-    i, j = (lax.broadcasted_iota(jnp.int32, (n, n), d) for d in (0, 1))
-    eye = jnp.where(i == j, 1.0, 0.0)
-    diagonal = jnp.where(i == j, gram[...], 0.0)
-    down = lax.rsqrt(jnp.sum(diagonal, axis=1, keepdims=True))
-    across = lax.rsqrt(jnp.sum(diagonal, axis=0, keepdims=True))
-    a[...] = gram[...] * down * across
-    first = jnp.where(i == j, 0.0, a[...])
-    w[...] = eye - tri_half(first)
-
-    def step(state):
-        count, _ = state
-        left = w[...]
-        e = mm(mm(left, a[...], NN, HI), left, NT, HI) - eye
-        w[...] = left - mm(tri_half(e), left, NN, HI)
-        return count + 1, jnp.max(jnp.abs(e))
-
-    _, worst = lax.while_loop(lambda t: (t[0] < 12) & ~(t[1] < 4e-4), step, (0, jnp.float32(1.0)))
-    inv_o[...] = w[...] * across
-
-    @pl.when(~(worst < 4e-4))
-    def _():
-        s[:, :n] = gram[...]
-        s[:, n:] = eye
-        row = lax.broadcasted_iota(jnp.int32, (n, 1), 0)
-
-        def eliminate(k, _):
-            line = s[pl.ds(k, 1), :]
-            column = jnp.sum(jnp.where(j == k, s[:, :n], 0.0), axis=1, keepdims=True)
-            pivot = jnp.sum(jnp.where(row == k, column, 0.0), axis=0, keepdims=True)
-            s[...] = s[...] - jnp.where(row > k, column / pivot, 0.0) * line
-            return 0
-
-        lax.fori_loop(0, n, eliminate, 0)
-        pivots = jnp.sum(jnp.where(i == j, s[:, :n], 0.0), axis=1, keepdims=True)
-        inv_o[...] = s[:, n:] / jnp.sqrt(pivots)
-
-
 def vmem(*shape, dtype=f32):
     return pltpu.VMEM(shape, dtype)
 
@@ -312,30 +336,35 @@
     rows, hid = mom.shape
     part, kr, nb = nx * nr, RANK // nr, BATCH // nr
     half = hid // ng
+
+    def piece(n):
+        return n, RANK // part + 1, RANK // 2
+
     left, gram, base, bufh = call(
         functools.partial(left_kernel, sizes),
         "hhhhh",
-        [((rows, RANK), bf16, "v"), ((RANK, RANK), f32, "v"), ((2, nb, half), f32, "v"), ((rows, hid), bf16, "v")],
+        [((rows, RANK), bf16, "v"), ((RANK + 8, RANK // 2), f32, "v"), ((2, nb, half), f32, "v"), ((rows, hid), bf16, "v")],
         [
             vmem(rows, hid), vmem(rows, hid, dtype=bf16), vmem(kr, hid), vmem(*weights.shape), vmem(*tokens.shape, dtype=bf16),
             pltpu.SemaphoreType.DMA((5,)), vmem(nr, kr, hid, dtype=bf16),
             vmem(nx, rows // nx, RANK), vmem(nx, rows // nx, RANK, dtype=bf16), vmem(nx - 1, rows // nx, RANK, dtype=bf16),
             vmem(nz, rows // nc, RANK), vmem(nz, rows // nc, RANK, dtype=bf16), vmem(nz - 1, rows // nc, RANK, dtype=bf16),
             vmem(nx, nz, rows // nc, RANK, dtype=bf16),
-            vmem(part, RANK // part, RANK), vmem(part - 1, RANK // part, RANK), vmem(part, RANK // part, RANK),
+            vmem(*piece(part)), vmem(*piece(part - 1)), vmem(*piece(part)),
             vmem(nr, 2, nb, half), vmem(nr - 1, 2, nb, half),
             pairs(nr - 1), pairs(nx - 1), pairs(nz - 1), pairs(nz - 1), pairs(nx - 1), pairs(part - 1), pairs(part - 1),
             pairs(nr - 1),
         ],
         (mom, grad, fq, weights, tokens), 0, limit=52.3,
     )
-    (linv,) = call(
-        inverse_kernel, "v", [((RANK, RANK), f32, "v")],
-        [vmem(RANK, RANK), vmem(RANK, RANK), vmem(RANK, 2 * RANK)], (gram,),
+    square = ((RANK, RANK), f32, "v")
+    start = call(
+        start_kernel, "v", [square, square, ((8, RANK), f32, "v"), ((8, 128), f32, "v")],
+        [vmem(RANK, RANK), vmem(RANK, 2 * RANK)], (gram,),
     )
     lh, oth, rh, rho, norms, share, tl = call(
         functools.partial(right_kernel, sizes),
-        "vvvv",
+        "v" * 7,
         [
             ((rows, RANK), bf16, "v"), ((rows, RANK), bf16, "v"), ((RANK, hid), bf16, "v"), ((nr, kr, half), bf16, "v"),
             ((nr, ng, 1, 128), f32, "v"), ((kr, hid), f32, "v"), ((2, nb, RANK), bf16, "v"),
@@ -346,11 +375,11 @@
             vmem(nr - 1, kr, hid, dtype=bf16), vmem(nr, nb, RANK), vmem(nr, nb, RANK, dtype=bf16),
             vmem(nr - 1, nb, RANK, dtype=bf16), vmem(nb, RANK, dtype=bf16), vmem(nb, RANK, dtype=bf16),
             vmem(nr, kr, hid, dtype=bf16), vmem(kr, half, dtype=bf16), vmem(nr, kr, half, dtype=bf16),
-            vmem(1, 128), vmem(ng, nx, 1, 128), vmem(nz, ng, 1, 128), vmem(nr, ng, 1, 128),
+            vmem(1, 128), vmem(ng, nz, 1, 128), vmem(nx, ng, 1, 128), vmem(nr, ng, 1, 128),
             pairs(1), pairs(nr - 1), pairs(nr - 1), pairs(nz - 1), pairs(nx - 1), pairs(nr - 1), pairs(1), pairs(nr - 1),
-            pairs(ng * nx - 1), pairs(nz - 1), pairs(nr - 1), pairs(1),
+            pairs(ng * nz - 1), pairs(nx - 1), pairs(nr - 1), pairs(1),
         ],
-        (bufh, left, linv, tokens), 1,
+        (bufh, left, *start, tokens), 1,
     )
     mom_new, new, fac, hidden = call(
         last_kernel, "v" * 11,

time: 167 us -> 144 us (0.86)
  Pallas kernels: 164 us -> 141 us
    pallas_call x4, Pallas kernels: 164 us -> 141 us  [call(): pl.pallas_call(kernel, out_shape=[jax.ShapeDtypeStruct(s, t) for s, t, _...]
where the time goes in v3:
time: 144 us; the launch traced here: 143 us
  Pallas kernels  141 us (98%)
  local copies, waits for them, and re-layouts  1.8 us (1%)
    pallas_call x4, Pallas kernels, call(): pl.pallas_call(kernel, out_shape=[jax.ShapeDtypeStruct(s, t) for s, t, _...  141 us

profile of v3, /device:TPU:1, one launch (start us, length us, event | category | flops | bytes accessed | tf_op | source)
XLA Modules:
  0.0 143.5 jit_solution(7279327302187645133)
XLA Ops:
  0.6 0.0 copy-start.3
  0.6 0.9 copy-done.3
  1.6 0.0 copy-start.4
  1.6 0.8 copy-done.4
  2.4 0.0 copy-start.1
  2.4 52.2 %shard_map.84 = (bf16[512,256]{1,0:T(8,128)(2,1)S(1)}, f32[264,128]{1,0:T(8,128)S(1)}, f32[2,32,256]{2,1,0:T(8,128)S(1)}, bf16[512,512]{1,0:T(8,128)(2,1)S(1)}) custom-call(f32[512,512]{1,0:T(8,128)} %bitcast.9, bf16[512,512]{1,0:T(8,128)(2,1)} %bitcast.11, f32[32,512]{1,0:T(8,128)S(1)} %bitcast.13, f32[2,512,256]{2,1,0:T(8,128)} %w.1, ...), custom_call_target="tpu_custom_call" | custom-call | tf_op jit(solution)/shard_map/pallas_call | solution.py:322
  54.6 0.0 copy-start
  54.6 57.3 %shard_map.85 = (f32[256,256]{1,0:T(8,128)S(1)}, f32[256,256]{1,0:T(8,128)S(1)}, f32[8,256]{1,0:T(8,128)S(1)}, f32[8,128]{1,0:T(8,128)S(1)}) custom-call(f32[264,128]{1,0:T(8,128)S(1)} %get-tuple-element.26.packed), custom_call_target="tpu_custom_call" | custom-call | tf_op jit(solution)/shard_map/pallas_call | solution.py:322
  112.0 0.0 copy-start.2
  112.0 29.2 %shard_map.86 = (bf16[512,256]{1,0:T(8,128)(2,1)S(1)}, bf16[512,256]{1,0:T(8,128)(2,1)S(1)}, bf16[256,512]{1,0:T(8,128)(2,1)S(1)}, bf16[8,32,256]{2,1,0:T(8,128)...) custom-call(bf16[512,512]{1,0:T(8,128)(2,1)S(1)} %get-tuple-element.24.bufh, ...), custom_call_target="tpu_custom_call" | custom-call | tf_op jit(solution)/shard_map/pallas_call | solution.py:322
  141.2 0.0 copy-done.1
  141.2 0.0 copy-done
  141.2 0.0 copy-done.2
  141.2 2.3 %shard_map.87 = (f32[512,512]{1,0:T(8,128)}, f32[2,512,256]{2,1,0:T(8,128)}, f32[32,512]{1,0:T(8,128)}, bf16[32,256]{1,0:T(8,128)(2,1)}) custom-call(f32[512,512]{1,0:T(8,128)S(1)} %bitcast.10, bf16[512,512]{1,0:T(8,128)(2,1)S(1)} %bitcast.12, f32[2,512,256]{2,1,0:T(8,128)S(1)} %copy-done.1, f32[2,32,256]{2,1,0:T(8,128)S(1)} %get-tuple-element.23.base, ...), custom_call_target="tpu_custom_call" | custom-call | tf_op jit(solution)/shard_map/pallas_call | solution.py:322
Async XLA Ops:
  0.6 1.0 copy-start.3
  1.6 0.8 copy-start.4
  2.4 138.7 %copy-start.1 = (f32[2,512,256]{2,1,0:T(8,128)S(1)}, f32[2,512,256]{2,1,0:T(8,128)}, u32[]{:S(2)}) copy-start(f32[2,512,256]{2,1,0:T(8,128)} %w.1) | copy-start | bytes 3145732
  54.6 86.5 %copy-start = (f32[1,512,512]{2,1,0:T(8,128)S(1)}, f32[1,512,512]{2,1,0:T(8,128)}, u32[]{:S(2)}) copy-start(f32[1,512,512]{2,1,0:T(8,128)} %param.5) | copy-start | bytes 3145732
  112.0 29.2 %copy-start.2 = (bf16[1,512,512]{2,1,0:T(8,128)(2,1)S(1)}, bf16[1,512,512]{2,1,0:T(8,128)(2,1)}, u32[]{:S(2)}) copy-start(bf16[1,512,512]{2,1,0:T(8,128)(2,1)} %param.6) | copy-start | bytes 1572868

commit v4 on v3

--- a/solution.py
+++ b/solution.py
@@ -35,17 +35,46 @@
     return [i if d == 0 else i + d - jnp.where(i + d >= n, n, 0) for d in range(n)]
 
 
+def far_first(offsets, *rings):
+    def way(offset):
+        return sum(min(d, n - d) for d, n in zip(offset, rings))
+
+    return sorted((offset for offset in offsets if any(offset)), key=lambda offset: -way(offset))
+
+
 class Place:
     def __init__(self, sizes):
         self.nr, self.nc, self.ng = sizes
-        self.nx, self.nz = NX, self.nc // NX
+        self.nx, self.nz, self.ny = NX, self.nc // NX, self.nr // 2
         self.r, self.c, self.g = (lax.axis_index(a) for a in ("row", "col", "grp"))
         self.x, self.z = lax.rem(self.c, self.nx), lax.div(self.c, self.nx)
-        self.rs, self.xs, self.zs = around(self.r, self.nr), around(self.x, self.nx), around(self.z, self.nz)
-        self.gs = [self.g, 1 - self.g]
-
-    def at(self, dr=0, dx=0, dz=0, dg=0):
-        return (self.rs[dr], self.zs[dz] * self.nx + self.xs[dx], self.gs[dg])
+        self.core = lax.rem(self.r, 2)
+        self.xs = around(self.x, self.nx)
+        ys = around(lax.div(self.r, 2), self.ny)
+        self.rs = {(dy, dc): 2 * ys[dy] + (1 - self.core if dc else self.core) for dy in range(self.ny) for dc in range(2)}
+        self.row = far_first(self.rs, self.ny)
+        self.line = [(d,) for d in range(1, self.nx)]
+        self.line = [d for (d,) in far_first(self.line, self.nx)]
+        self.plane = far_first([(dx, *d) for dx in range(self.nx) for d in self.rs], self.nx, self.ny)
+        last = self.nz - 1
+        self.stack = [
+            jnp.where(
+                self.z <= last // 2,
+                last - k - jnp.where(last - k <= self.z, 1, 0),
+                k + jnp.where(k >= self.z, 1, 0),
+            )
+            for k in range(last)
+        ]
+        around_both = around(self.g * self.nz + self.z, self.ng * self.nz)
+        self.ring = [around_both[d] for (d,) in far_first([(d,) for d in range(len(around_both))], len(around_both))]
+
+    def at(self, row=(0, 0), dx=0, z=None, g=None):
+        z = self.z if z is None else z
+        return (self.rs[row], z * self.nx + self.xs[dx], self.g if g is None else g)
+
+    def up(self, k):
+        g = jnp.where(self.ring[k] >= self.nz, 1, 0)
+        return self.at(z=self.ring[k] - g * self.nz, g=g)
 
 
 def greet(partners):
@@ -55,12 +84,25 @@
     return lambda: pl.semaphore_wait(barrier, len(partners))
 
 
+def remote(src, dst, sent, received, device):
+    return pltpu.make_async_remote_copy(
+        src_ref=src, dst_ref=dst, send_sem=sent, recv_sem=received, device_id=device, device_id_type=MESH
+    )
+
+
 def send(src, dst, sems, k, device):
-    copy = pltpu.make_async_remote_copy(
-        src_ref=src, dst_ref=dst, send_sem=sems.at[0, k], recv_sem=sems.at[1, k], device_id=device, device_id_type=MESH
-    )
+    copy = remote(src, dst, sems.at[0, k], sems.at[1, k], device)
     copy.start()
     return copy
+
+
+def send_line(pick, slot, sems, at):
+    waits = []
+    for k, other in enumerate(at.stack):
+        device = at.at(z=other)
+        remote(pick(other), slot(at.z), sems.at[0, k], sems.at[1, at.z], device).start()
+        waits.append(remote(pick(other), slot(other), sems.at[0, k], sems.at[1, other], device))
+    return waits
 
 
 def arrived(copies):
@@ -73,8 +115,7 @@
                 s_q, s_x, s_z, s_az, s_ax, s_g, s_ag, s_p):
     at = Place(sizes)
     nr, nx, nz = at.nr, at.nx, at.nz
-    plane = [(dx, dr) for dx in range(nx) for dr in range(nr) if dx or dr]
-    ready = greet([at.at(dr=dr, dx=dx) for dx, dr in plane] + [at.at(dz=d) for d in range(1, nz)])
+    ready = greet([at.at(z=other) for other in at.stack] + [at.at(row=d[1:], dx=d[0]) for d in at.plane])
     r, x, z = at.r, at.x, at.z
     loads = [
         pltpu.make_async_copy(a, b, s_in.at[k])
@@ -85,14 +126,14 @@
     loads[0].wait()
     qbuf[r] = fq[...].astype(bf16)
     ready()
-    got_q = [send(qbuf.at[r], qbuf.at[r], s_q, d - 1, at.at(dr=d)) for d in range(1, nr)]
+    got_q = [send(qbuf.at[r], qbuf.at[r], s_q, k, at.at(row=d)) for k, d in enumerate(at.row)]
     loads[1].wait()
     loads[2].wait()
     bufh[...] = (mom[...] + grad[...].astype(f32)).astype(bf16)
     arrived(got_q)
     part[...] = mm(bufh[...], qbuf[...].reshape(RANK, -1), NT).reshape(part.shape)
     partb[...] = part[...].astype(bf16)
-    got_x = [send(partb.at[at.xs[d]], rx.at[d - 1], s_x, d - 1, at.at(dx=d)) for d in range(1, nx)]
+    got_x = [send(partb.at[at.xs[d]], rx.at[k], s_x, k, at.at(dx=d)) for k, d in enumerate(at.line)]
     loads[3].wait()
     loads[4].wait()
     for p in range(2):
@@ -102,11 +143,12 @@
     arrived(got_x)
     sx[...] = (part[x] + jnp.sum(rx[...].astype(f32), axis=0)).reshape(sx.shape)
     sxb[...] = sx[...].astype(bf16)
-    got_z = [send(sxb.at[at.zs[d]], rz.at[d - 1], s_z, d - 1, at.at(dz=d)) for d in range(1, nz)]
-    got_p = [send(pre.at[at.rs[d]], rpre.at[d - 1], s_p, d - 1, at.at(dr=d)) for d in range(1, nr)]
+    rz[z] = jnp.zeros(rz.shape[1:], bf16)
+    got_z = send_line(lambda other: sxb.at[other], lambda place: rz.at[place], s_z, at)
+    got_p = [send(pre.at[at.rs[d]], rpre.at[k], s_p, k, at.at(row=d)) for k, d in enumerate(at.row)]
     arrived(got_z)
     l512[x, z] = (sx[z] + jnp.sum(rz[...].astype(f32), axis=0)).astype(bf16)
-    got_az = [send(l512.at[x, z], l512.at[x, z], s_az, d - 1, at.at(dz=d)) for d in range(1, nz)]
+    got_az = send_line(lambda other: l512.at[x, z], lambda place: l512.at[x, place], s_az, at)
     arrived(got_az)
     rows = l512[x].reshape(-1, RANK)
     gram = mm(rows, rows, TN)
@@ -119,14 +161,14 @@
         jnp.sum(jnp.where(i == j, gram[h:, h:], 0.0), axis=0, keepdims=True), (gp.shape[0], 1, h)
     )
     got_g = []
-    for k, (dx, dr) in enumerate(plane):
-        m = at.xs[dx] * nr + at.rs[dr]
-        got_g.append(send(gp.at[m], rg.at[k], s_g, k, at.at(dr=dr, dx=dx)))
-    got_ax = [send(l512.at[x], l512.at[x], s_ax, d - 1, at.at(dx=d)) for d in range(1, nx)]
+    for k, (dx, *d) in enumerate(at.plane):
+        m = at.xs[dx] * nr + at.rs[*d]
+        got_g.append(send(gp.at[m], rg.at[k], s_g, k, at.at(row=(*d,), dx=dx)))
+    got_ax = [send(l512.at[x], l512.at[x], s_ax, k, at.at(dx=d)) for k, d in enumerate(at.line)]
     arrived(got_g)
     m = x * nr + r
     gf[m] = gp[m] + jnp.sum(rg[...], axis=0)
-    got_ag = [send(gf.at[m], gf.at[m], s_ag, k, at.at(dr=dr, dx=dx)) for k, (dx, dr) in enumerate(plane)]
+    got_ag = [send(gf.at[m], gf.at[m], s_ag, k, at.at(row=d[1:], dx=d[0])) for k, d in enumerate(at.plane)]
     arrived(got_p)
     base_o[...] = pre[r] + jnp.sum(rpre[...], axis=0)
     arrived(got_ax)
@@ -192,20 +234,23 @@
         near_o[...] = jnp.zeros(near_o.shape, f32)
 
 
-def right_kernel(sizes, bufh, left, a, w, across, near, tok, lh_o, oth_o, rh_o, rho_o, nb_o, share_o, tl_o,
-                 lh, oth, rt, rtb, rrt, tl, tlb, rtl, tls, tlo, rh, sho, rho, sq, sqz, sqx, nb,
+def right_kernel(sizes, bufh, left, a, w, across, near, tok, mom_h, grad_h, mom_o, lh_o, oth_o, rh_o, rho_o, nb_o, share_o, tl_o,
+                 mom, grad, s_in, lh, oth, rt, rtb, rrt, tl, tlb, rtl, tls, tlo, rh, sho, rho, sq, sqz, sqx, nb,
                  s_l, s_rt, s_tl, s_lz, s_lx, s_rh, s_sh, s_ro, s_sq, s_sx, s_nb, s_to):
     at = Place(sizes)
     nr, nx, nz, ng = at.nr, at.nx, at.nz, at.ng
     r, c, g, x, z = at.r, at.c, at.g, at.x, at.z
-    line_up = [(dz, dg) for dz in range(nz) for dg in range(ng) if dz or dg]
+    upwards = range(len(at.ring))
     ready = greet(
-        [at.at(dr=d) for d in range(1, nr)] + [at.at(dx=d) for d in range(1, nx)] + [at.at(dz=dz, dg=dg) for dz, dg in line_up]
+        [at.up(k) for k in upwards] + [at.at(row=d) for d in at.row] + [at.at(dx=d) for d in at.line]
     )
     o = 1 - g
     kr = RANK // nr
     half = sho.shape[1]
 
+    loads = [pltpu.make_async_copy(mom_h, mom, s_in.at[0]), pltpu.make_async_copy(grad_h, grad, s_in.at[1])]
+    for load in loads:
+        load.start()
     inverse = w[...]
     for _ in range(3):
         error = jnp.where(near[:1, :1] > 0, tri_half(residual(inverse, a[...], HI)), 0.0)
@@ -216,43 +261,46 @@
     left_h = (mm(left[...], high, NT) + mm(left[...], low, NT)).astype(bf16)
     lh[...] = left_h.reshape(lh.shape)
     ready()
-    got_l = [send(lh.at[x, z], oth.at[x, z], s_l, 0, at.at(dg=1))]
+    got_l = [send(lh.at[x, z], oth.at[x, z], s_l, 0, at.at(g=o))]
     rt[...] = mm(left_h, bufh[...], TN).reshape(rt.shape)
     rtb[...] = rt[...].astype(bf16)
-    got_rt = [send(rtb.at[at.rs[d]], rrt.at[d - 1], s_rt, d - 1, at.at(dr=d)) for d in range(1, nr)]
+    got_rt = [send(rtb.at[at.rs[d]], rrt.at[k], s_rt, k, at.at(row=d)) for k, d in enumerate(at.row)]
     tl[...] = mm(tok[...], left_h).reshape(tl.shape)
     tlb[...] = tl[...].astype(bf16)
-    got_tl = [send(tlb.at[at.rs[d]], rtl.at[d - 1], s_tl, d - 1, at.at(dr=d)) for d in range(1, nr)]
+    got_tl = [send(tlb.at[at.rs[d]], rtl.at[k], s_tl, k, at.at(row=d)) for k, d in enumerate(at.row)]
     arrived(got_rt)
     share = rt[r] + jnp.sum(rrt[...].astype(f32), axis=0)
     share_o[...] = share
     rh[r] = share.astype(bf16)
     sho[...] = share_o[:, pl.ds(pl.multiple_of(o * half, half), half)].astype(bf16)
-    got_sh = [send(sho, rho.at[r], s_sh, 0, at.at(dg=1))]
+    got_sh = [send(sho, rho.at[r], s_sh, 0, at.at(g=o))]
     eye = lax.broadcasted_iota(jnp.int32, (kr, 128), 0) == lax.broadcasted_iota(jnp.int32, (kr, 128), 1)
     squares = jnp.sum(share * share, axis=1, keepdims=True)
     line = jnp.sum(jnp.where(eye, squares, 0.0), axis=0, keepdims=True)
     sqz[g, z] = line
     sq[...] = line
-    got_sq = [send(sq, sqz.at[g, z], s_sq, k, at.at(dz=dz, dg=dg)) for k, (dz, dg) in enumerate(line_up)]
-    got_rh = [send(rh.at[r], rh.at[r], s_rh, d - 1, at.at(dr=d)) for d in range(1, nr)]
+    got_sq = [send(sq, sqz.at[g, z], s_sq, k, at.up(k)) for k in upwards]
+    got_rh = [send(rh.at[r], rh.at[r], s_rh, k, at.at(row=d)) for k, d in enumerate(at.row)]
     arrived(got_tl)
     tls[...] = (tl[r] + jnp.sum(rtl[...].astype(f32), axis=0)).astype(bf16)
-    got_to = [send(tls, tlo, s_to, 0, at.at(dg=1))]
+    got_to = [send(tls, tlo, s_to, 0, at.at(g=o))]
     arrived(got_l)
-    got_lz = [send(oth.at[x, z], oth.at[x, z], s_lz, d - 1, at.at(dz=d)) for d in range(1, nz)]
+    got_lz = send_line(lambda other: oth.at[x, z], lambda place: oth.at[x, place], s_lz, at)
     arrived(got_sh)
-    got_ro = [send(rho.at[r], rho.at[r], s_ro, d - 1, at.at(dr=d)) for d in range(1, nr)]
+    got_ro = [send(rho.at[r], rho.at[r], s_ro, k, at.at(row=d)) for k, d in enumerate(at.row)]
     arrived(got_sq)
     sqx[x] = jnp.sum(sqz[...], axis=1)
-    got_sx = [send(sqx.at[x], sqx.at[x], s_sx, d - 1, at.at(dx=d)) for d in range(1, nx)]
+    got_sx = [send(sqx.at[x], sqx.at[x], s_sx, k, at.at(dx=d)) for k, d in enumerate(at.line)]
     arrived(got_lz)
-    got_lx = [send(oth.at[x], oth.at[x], s_lx, d - 1, at.at(dx=d)) for d in range(1, nx)]
+    got_lx = [send(oth.at[x], oth.at[x], s_lx, k, at.at(dx=d)) for k, d in enumerate(at.line)]
     arrived(got_sx)
     nb[r] = jnp.sum(sqx[...], axis=0)
-    got_nb = [send(nb.at[r], nb.at[r], s_nb, d - 1, at.at(dr=d)) for d in range(1, nr)]
+    got_nb = [send(nb.at[r], nb.at[r], s_nb, k, at.at(row=d)) for k, d in enumerate(at.row)]
     lh_o[...] = lh[...].reshape(lh_o.shape)
+    for load in loads:
+        load.wait()
     arrived(got_rh)
+    mom_o[...] = mom[...] + grad[...].astype(f32) - FEEDBACK * mm(left_h, rh[...].reshape(RANK, -1))
     rh_o[...] = rh[...].reshape(rh_o.shape)
     arrived(got_lx)
     oth_o[...] = oth[...].reshape(oth_o.shape)
@@ -268,7 +316,7 @@
             copy.wait_send()
 
 
-def last_kernel(mom, grad, w, base, lh, oth, rh, rho, nb, share, tl, mom_h, new_h, fac_o, hid_o, mom_v, new_v, sems):
+def last_kernel(mom, w, base, lh, oth, rh, rho, nb, share, tl, mom_h, new_h, fac_o, hid_o, new_v, sems):
     r, g = lax.axis_index("row"), lax.axis_index("grp")
     o = 1 - g
     nr, kr, half = rho.shape
@@ -280,10 +328,7 @@
         copies.append(pltpu.make_async_copy(src, dst, sems.at[len(copies)]))
         copies[-1].start()
 
-    for k in range(CHUNKS):
-        at = pl.ds(k * chunk, chunk)
-        mom_v[at] = mom[at] + grad[at].astype(f32) - FEEDBACK * mm(lh[at], rh[...])
-        out(mom_v.at[at], mom_h.at[at])
+    out(mom, mom_h)
     eye = lax.broadcasted_iota(jnp.int32, (kr, 128), 0) == lax.broadcasted_iota(jnp.int32, (kr, 128), 1)
 
     def columns(norms):
@@ -348,11 +393,11 @@
             vmem(rows, hid), vmem(rows, hid, dtype=bf16), vmem(kr, hid), vmem(*weights.shape), vmem(*tokens.shape, dtype=bf16),
             pltpu.SemaphoreType.DMA((5,)), vmem(nr, kr, hid, dtype=bf16),
             vmem(nx, rows // nx, RANK), vmem(nx, rows // nx, RANK, dtype=bf16), vmem(nx - 1, rows // nx, RANK, dtype=bf16),
-            vmem(nz, rows // nc, RANK), vmem(nz, rows // nc, RANK, dtype=bf16), vmem(nz - 1, rows // nc, RANK, dtype=bf16),
+            vmem(nz, rows // nc, RANK), vmem(nz, rows // nc, RANK, dtype=bf16), vmem(nz, rows // nc, RANK, dtype=bf16),
             vmem(nx, nz, rows // nc, RANK, dtype=bf16),
             vmem(*piece(part)), vmem(*piece(part - 1)), vmem(*piece(part)),
             vmem(nr, 2, nb, half), vmem(nr - 1, 2, nb, half),
-            pairs(nr - 1), pairs(nx - 1), pairs(nz - 1), pairs(nz - 1), pairs(nx - 1), pairs(part - 1), pairs(part - 1),
+            pairs(nr - 1), pairs(nx - 1), pairs(nz), pairs(nz), pairs(nx - 1), pairs(part - 1), pairs(part - 1),
             pairs(nr - 1),
         ],
         (mom, grad, fq, weights, tokens), 0, limit=52.3,
@@ -362,30 +407,30 @@
         start_kernel, "v", [square, square, ((8, RANK), f32, "v"), ((8, 128), f32, "v")],
         [vmem(RANK, RANK), vmem(RANK, 2 * RANK)], (gram,),
     )
-    lh, oth, rh, rho, norms, share, tl = call(
+    mom_new, lh, oth, rh, rho, norms, share, tl = call(
         functools.partial(right_kernel, sizes),
-        "v" * 7,
+        "v" * 7 + "hh",
         [
-            ((rows, RANK), bf16, "v"), ((rows, RANK), bf16, "v"), ((RANK, hid), bf16, "v"), ((nr, kr, half), bf16, "v"),
+            ((rows, hid), f32, "v"), ((rows, RANK), bf16, "v"), ((rows, RANK), bf16, "v"), ((RANK, hid), bf16, "v"), ((nr, kr, half), bf16, "v"),
             ((nr, ng, 1, 128), f32, "v"), ((kr, hid), f32, "v"), ((2, nb, RANK), bf16, "v"),
         ],
         [
-            vmem(nx, nz, rows // nc, RANK, dtype=bf16),
-            vmem(nx, nz, rows // nc, RANK, dtype=bf16), vmem(nr, kr, hid), vmem(nr, kr, hid, dtype=bf16),
+            vmem(rows, hid), vmem(rows, hid, dtype=bf16), pltpu.SemaphoreType.DMA((2,)),
+            vmem(nx, nz, rows // nc, RANK, dtype=bf16), vmem(nx, nz, rows // nc, RANK, dtype=bf16), vmem(nr, kr, hid), vmem(nr, kr, hid, dtype=bf16),
             vmem(nr - 1, kr, hid, dtype=bf16), vmem(nr, nb, RANK), vmem(nr, nb, RANK, dtype=bf16),
             vmem(nr - 1, nb, RANK, dtype=bf16), vmem(nb, RANK, dtype=bf16), vmem(nb, RANK, dtype=bf16),
             vmem(nr, kr, hid, dtype=bf16), vmem(kr, half, dtype=bf16), vmem(nr, kr, half, dtype=bf16),
             vmem(1, 128), vmem(ng, nz, 1, 128), vmem(nx, ng, 1, 128), vmem(nr, ng, 1, 128),
-            pairs(1), pairs(nr - 1), pairs(nr - 1), pairs(nz - 1), pairs(nx - 1), pairs(nr - 1), pairs(1), pairs(nr - 1),
+            pairs(1), pairs(nr - 1), pairs(nr - 1), pairs(nz), pairs(nx - 1), pairs(nr - 1), pairs(1), pairs(nr - 1),
             pairs(ng * nz - 1), pairs(nx - 1), pairs(nr - 1), pairs(1),
         ],
-        (bufh, left, *start, tokens), 1,
+        (bufh, left, *start, tokens, mom, grad), 1,
     )
     mom_new, new, fac, hidden = call(
-        last_kernel, "v" * 11,
+        last_kernel, "v" * 10,
         [((rows, hid), f32, "h"), (weights.shape, f32, "h"), ((kr, hid), f32, "v"), ((nb, half), bf16, "v")],
-        [vmem(rows, hid), vmem(*weights.shape), pltpu.SemaphoreType.DMA((3 * CHUNKS,))],
-        (mom, grad, weights, base, lh, oth, rh, rho, norms, share, tl),
+        [vmem(*weights.shape), pltpu.SemaphoreType.DMA((2 * CHUNKS + 1,))],
+        (mom_new, weights, base, lh, oth, rh, rho, norms, share, tl),
     )
     return mom_new[None], fac.T[None], new, hidden
 

time: 144 us -> 140 us (0.972)
  Pallas kernels: 141 us -> 138 us
    pallas_call x4, Pallas kernels: 141 us -> 138 us  [call(): pl.pallas_call(kernel, out_shape=[jax.ShapeDtypeStruct(s, t) for s, t, _...]
where the time goes in v4:
time: 140 us
  Pallas kernels  138 us (99%)
  local copies, waits for them, and re-layouts  1.8 us (1%)
    pallas_call x4, Pallas kernels, call(): pl.pallas_call(kernel, out_shape=[jax.ShapeDtypeStruct(s, t) for s, t, _...  138 us

profile of v4, /device:TPU:1, one launch (start us, length us, event | category | flops | bytes accessed | tf_op | source)
XLA Modules:
  0.0 140.2 jit_solution(12107786134283401025)
XLA Ops:
  0.6 0.0 copy-start.3
  0.6 0.9 copy-done.3
  1.6 0.0 copy-start.4
  1.6 0.8 copy-done.4
  2.4 0.0 copy-start.1
  2.4 0.0 copy-start.2
  2.4 49.9 %shard_map.84 = (bf16[512,256]{1,0:T(8,128)(2,1)S(1)}, f32[264,128]{1,0:T(8,128)S(1)}, f32[2,32,256]{2,1,0:T(8,128)S(1)}, bf16[512,512]{1,0:T(8,128)(2,1)S(1)}) custom-call(f32[512,512]{1,0:T(8,128)} %bitcast.9, bf16[512,512]{1,0:T(8,128)(2,1)} %bitcast.11, f32[32,512]{1,0:T(8,128)S(1)} %bitcast.13, f32[2,512,256]{2,1,0:T(8,128)} %w.1, ...), custom_call_target="tpu_custom_call" | custom-call | tf_op jit(solution)/shard_map/pallas_call | solution.py:367
  52.4 57.3 %shard_map.85 = (f32[256,256]{1,0:T(8,128)S(1)}, f32[256,256]{1,0:T(8,128)S(1)}, f32[8,256]{1,0:T(8,128)S(1)}, f32[8,128]{1,0:T(8,128)S(1)}) custom-call(f32[264,128]{1,0:T(8,128)S(1)} %get-tuple-element.26.packed), custom_call_target="tpu_custom_call" | custom-call | tf_op jit(solution)/shard_map/pallas_call | solution.py:367
  109.7 0.0 copy-done.1
  109.7 0.0 copy-done.2
  109.7 0.0 copy-start
  109.7 28.4 %shard_map.86 = (f32[512,512]{1,0:T(8,128)S(1)}, bf16[512,256]{1,0:T(8,128)(2,1)S(1)}, bf16[512,256]{1,0:T(8,128)(2,1)S(1)}, bf16[256,512]{1,0:T(8,128)(2,1)S(1)...) custom-call(bf16[512,512]{1,0:T(8,128)(2,1)S(1)} %get-tuple-element., ...), custom_call_target="tpu_custom_call" | custom-call | tf_op jit(solution)/shard_map/pallas_call | solution.py:367
  138.2 0.0 copy-done
  138.2 2.0 %shard_map.87 = (f32[512,512]{1,0:T(8,128)}, f32[2,512,256]{2,1,0:T(8,128)}, f32[32,512]{1,0:T(8,128)}, bf16[32,256]{1,0:T(8,128)(2,1)}) custom-call(f32[512,512]{1,0:T(8,128)S(1)} %get-tuple-element.31.mom, f32[2,512,256]{2,1,0:T(8,128)S(1)} %copy-done, f32[2,32,256]{2,1,0:T(8,128)S(1)} %get-tuple-element.32.base, ...), custom_call_target="tpu_custom_call" | custom-call | tf_op jit(solution)/shard_map/pallas_call | solution.py:367
Async XLA Ops:
  0.6 1.0 copy-start.3
  1.6 0.8 copy-start.4
  2.4 107.3 %copy-start.1 = (f32[1,512,512]{2,1,0:T(8,128)S(1)}, f32[1,512,512]{2,1,0:T(8,128)}, u32[]{:S(2)}) copy-start(f32[1,512,512]{2,1,0:T(8,128)} %param.5) | copy-start | bytes 3145732
  2.4 107.3 %copy-start.2 = (bf16[1,512,512]{2,1,0:T(8,128)(2,1)S(1)}, bf16[1,512,512]{2,1,0:T(8,128)(2,1)}, u32[]{:S(2)}) copy-start(bf16[1,512,512]{2,1,0:T(8,128)(2,1)} %param.6) | copy-start | bytes 1572868
  109.7 28.5 %copy-start = (f32[2,512,256]{2,1,0:T(8,128)S(1)}, f32[2,512,256]{2,1,0:T(8,128)}, u32[]{:S(2)}) copy-start(f32[2,512,256]{2,1,0:T(8,128)} %w.1) | copy-start | bytes 3145732

commit v5 on v4

--- a/solution.py
+++ b/solution.py
@@ -235,14 +235,14 @@
 
 
 def right_kernel(sizes, bufh, left, a, w, across, near, tok, mom_h, grad_h, mom_o, lh_o, oth_o, rh_o, rho_o, nb_o, share_o, tl_o,
-                 mom, grad, s_in, lh, oth, rt, rtb, rrt, tl, tlb, rtl, tls, tlo, rh, sho, rho, sq, sqz, sqx, nb,
-                 s_l, s_rt, s_tl, s_lz, s_lx, s_rh, s_sh, s_ro, s_sq, s_sx, s_nb, s_to):
+                 mom, grad, s_in, lh, oth, rt, rtb, rrt, tl, tlb, rtl, tls, tlo, rh, sho, rho, sq, sqz, sqx,
+                 s_l, s_rt, s_tl, s_lz, s_lx, s_rh, s_sh, s_ro, s_sq, s_nb, s_to):
     at = Place(sizes)
     nr, nx, nz, ng = at.nr, at.nx, at.nz, at.ng
     r, c, g, x, z = at.r, at.c, at.g, at.x, at.z
     upwards = range(len(at.ring))
     ready = greet(
-        [at.up(k) for k in upwards] + [at.at(row=d) for d in at.row] + [at.at(dx=d) for d in at.line]
+        [at.up(k) for k in upwards] + [at.at(row=d[1:], dx=d[0]) for d in at.plane]
     )
     o = 1 - g
     kr = RANK // nr
@@ -280,22 +280,19 @@
     sqz[g, z] = line
     sq[...] = line
     got_sq = [send(sq, sqz.at[g, z], s_sq, k, at.up(k)) for k in upwards]
+    arrived(got_l)
+    got_lz = send_line(lambda other: oth.at[x, z], lambda place: oth.at[x, place], s_lz, at)
     got_rh = [send(rh.at[r], rh.at[r], s_rh, k, at.at(row=d)) for k, d in enumerate(at.row)]
     arrived(got_tl)
     tls[...] = (tl[r] + jnp.sum(rtl[...].astype(f32), axis=0)).astype(bf16)
     got_to = [send(tls, tlo, s_to, 0, at.at(g=o))]
-    arrived(got_l)
-    got_lz = send_line(lambda other: oth.at[x, z], lambda place: oth.at[x, place], s_lz, at)
     arrived(got_sh)
     got_ro = [send(rho.at[r], rho.at[r], s_ro, k, at.at(row=d)) for k, d in enumerate(at.row)]
-    arrived(got_sq)
-    sqx[x] = jnp.sum(sqz[...], axis=1)
-    got_sx = [send(sqx.at[x], sqx.at[x], s_sx, k, at.at(dx=d)) for k, d in enumerate(at.line)]
     arrived(got_lz)
     got_lx = [send(oth.at[x], oth.at[x], s_lx, k, at.at(dx=d)) for k, d in enumerate(at.line)]
-    arrived(got_sx)
-    nb[r] = jnp.sum(sqx[...], axis=0)
-    got_nb = [send(nb.at[r], nb.at[r], s_nb, k, at.at(row=d)) for k, d in enumerate(at.row)]
+    arrived(got_sq)
+    sqx[x, r] = jnp.sum(sqz[...], axis=1)
+    got_nb = [send(sqx.at[x, r], sqx.at[x, r], s_nb, k, at.at(row=d[1:], dx=d[0])) for k, d in enumerate(at.plane)]
     lh_o[...] = lh[...].reshape(lh_o.shape)
     for load in loads:
         load.wait()
@@ -305,13 +302,13 @@
     arrived(got_lx)
     oth_o[...] = oth[...].reshape(oth_o.shape)
     arrived(got_nb)
-    nb_o[...] = nb[...]
+    nb_o[...] = jnp.sum(sqx[...], axis=0)
     arrived(got_ro)
     rho_o[...] = rho[...]
     arrived(got_to)
     tl_o[0] = tls[...]
     tl_o[1] = tlo[...]
-    for copies in (got_l, got_rt, got_tl, got_lz, got_sh, got_sq, got_sx, got_rh, got_lx, got_nb, got_ro, got_to):
+    for copies in (got_l, got_rt, got_tl, got_lz, got_sh, got_sq, got_rh, got_lx, got_nb, got_ro, got_to):
         for copy in copies:
             copy.wait_send()
 
@@ -400,7 +397,7 @@
             pairs(nr - 1), pairs(nx - 1), pairs(nz), pairs(nz), pairs(nx - 1), pairs(part - 1), pairs(part - 1),
             pairs(nr - 1),
         ],
-        (mom, grad, fq, weights, tokens), 0, limit=52.3,
+        [pltpu.with_memory_space_constraint(a, pltpu.HBM) for a in (mom, grad, fq, weights, tokens)], 0,
     )
     square = ((RANK, RANK), f32, "v")
     start = call(
@@ -420,9 +417,9 @@
             vmem(nr - 1, kr, hid, dtype=bf16), vmem(nr, nb, RANK), vmem(nr, nb, RANK, dtype=bf16),
             vmem(nr - 1, nb, RANK, dtype=bf16), vmem(nb, RANK, dtype=bf16), vmem(nb, RANK, dtype=bf16),
             vmem(nr, kr, hid, dtype=bf16), vmem(kr, half, dtype=bf16), vmem(nr, kr, half, dtype=bf16),
-            vmem(1, 128), vmem(ng, nz, 1, 128), vmem(nx, ng, 1, 128), vmem(nr, ng, 1, 128),
+            vmem(1, 128), vmem(ng, nz, 1, 128), vmem(nx, nr, ng, 1, 128),
             pairs(1), pairs(nr - 1), pairs(nr - 1), pairs(nz), pairs(nx - 1), pairs(nr - 1), pairs(1), pairs(nr - 1),
-            pairs(ng * nz - 1), pairs(nx - 1), pairs(nr - 1), pairs(1),
+            pairs(ng * nz - 1), pairs(part - 1), pairs(1),
         ],
         (bufh, left, *start, tokens, mom, grad), 1,
     )

time: 140 us -> 139 us (level)
  local copies, waits for them, and re-layouts: 1.8 us -> 0.02 us
    unnamed x10 -> x8, local copies, waits for them, and re-layouts: 1.8 us -> 0.02 us
where the time goes in v5:
time: 139 us
  Pallas kernels  138 us (99%)
    pallas_call x4, Pallas kernels, call(): pl.pallas_call(kernel, out_shape=[jax.ShapeDtypeStruct(s, t) for s, t, _...  138 us

profile of v5, /device:TPU:1, one launch (start us, length us, event | category | flops | bytes accessed | tf_op | source)
XLA Modules:
  0.0 139.1 jit_solution(12124535006578613688)
XLA Ops:
  0.6 0.0 copy-start.1
  0.6 0.0 copy-start.2
  0.7 0.0 copy-start.3
  0.7 49.9 %shard_map.84 = (bf16[512,256]{1,0:T(8,128)(2,1)S(1)}, f32[264,128]{1,0:T(8,128)S(1)}, f32[2,32,256]{2,1,0:T(8,128)S(1)}, bf16[512,512]{1,0:T(8,128)(2,1)S(1)}) custom-call(f32[512,512]{1,0:T(8,128)} %bitcast.9, bf16[512,512]{1,0:T(8,128)(2,1)} %bitcast.11, f32[32,512]{1,0:T(8,128)} %bitcast.13, f32[2,512,256]{2,1,0:T(8,128)} %w.1, bf16[256,512]{1,0:T(8,128)(2,1)} %tok.1), custom_call_target="tpu_custom_call" | custom-call | tf_op jit(solution)/shard_map/pallas_call | solution.py:364
  50.6 57.3 %shard_map.85 = (f32[256,256]{1,0:T(8,128)S(1)}, f32[256,256]{1,0:T(8,128)S(1)}, f32[8,256]{1,0:T(8,128)S(1)}, f32[8,128]{1,0:T(8,128)S(1)}) custom-call(f32[264,128]{1,0:T(8,128)S(1)} %get-tuple-element.26.packed), custom_call_target="tpu_custom_call" | custom-call | tf_op jit(solution)/shard_map/pallas_call | solution.py:364
  107.9 0.0 copy-done.1
  107.9 0.0 copy-done.2
  107.9 0.0 copy-done.3
  108.0 0.0 copy-start
  108.0 29.1 %shard_map.86 = (f32[512,512]{1,0:T(8,128)S(1)}, bf16[512,256]{1,0:T(8,128)(2,1)S(1)}, bf16[512,256]{1,0:T(8,128)(2,1)S(1)}, bf16[256,512]{1,0:T(8,128)(2,1)S(1)...) custom-call(bf16[512,512]{1,0:T(8,128)(2,1)S(1)} %get-tuple-element., ...), custom_call_target="tpu_custom_call" | custom-call | tf_op jit(solution)/shard_map/pallas_call | solution.py:364
  137.0 0.0 copy-done
  137.0 2.0 %shard_map.87 = (f32[512,512]{1,0:T(8,128)}, f32[2,512,256]{2,1,0:T(8,128)}, f32[32,512]{1,0:T(8,128)}, bf16[32,256]{1,0:T(8,128)(2,1)}) custom-call(f32[512,512]{1,0:T(8,128)S(1)} %get-tuple-element.31.mom, f32[2,512,256]{2,1,0:T(8,128)S(1)} %copy-done, f32[2,32,256]{2,1,0:T(8,128)S(1)} %get-tuple-element.32.base, ...), custom_call_target="tpu_custom_call" | custom-call | tf_op jit(solution)/shard_map/pallas_call | solution.py:364
Async XLA Ops:
  0.6 107.3 %copy-start.1 = (f32[1,512,512]{2,1,0:T(8,128)S(1)}, f32[1,512,512]{2,1,0:T(8,128)}, u32[]{:S(2)}) copy-start(f32[1,512,512]{2,1,0:T(8,128)} %param.5) | copy-start | bytes 3145732
  0.6 107.3 %copy-start.2 = (bf16[1,512,512]{2,1,0:T(8,128)(2,1)S(1)}, bf16[1,512,512]{2,1,0:T(8,128)(2,1)}, u32[]{:S(2)}) copy-start(bf16[1,512,512]{2,1,0:T(8,128)(2,1)} %param.6) | copy-start | bytes 1572868
  0.7 107.3 %copy-start.3 = (bf16[256,512]{1,0:T(8,128)(2,1)S(1)}, bf16[256,512]{1,0:T(8,128)(2,1)}, u32[]{:S(2)}) copy-start(bf16[256,512]{1,0:T(8,128)(2,1)} %tok.1) | copy-start | bytes 786436
  108.0 29.1 %copy-start = (f32[2,512,256]{2,1,0:T(8,128)S(1)}, f32[2,512,256]{2,1,0:T(8,128)}, u32[]{:S(2)}) copy-start(f32[2,512,256]{2,1,0:T(8,128)} %w.1) | copy-start | bytes 3145732

commit v6 on v4

--- a/solution.py
+++ b/solution.py
@@ -16,7 +16,7 @@
 EPSILON = 1e-06
 STEP = 0.4 * math.sqrt(max(D, HID))
 CHUNKS = 4
-NEAR = 0.16
+NEAR = 0.1
 NX = 4
 
 f32, bf16 = jnp.float32, jnp.bfloat16
@@ -209,8 +209,8 @@
     across_o[...] = jnp.broadcast_to(across, across_o.shape)
     w = eye - tri_half(jnp.where(i == j, 0.0, a))
     w = w - mm(tri_half(residual(w, a)), w)
-    w_o[...] = w
     e = residual(w, a)
+    w_o[...] = w - mm(tri_half(e), w)
     far = jnp.sum(e * e)
     near_o[...] = jnp.ones(near_o.shape, f32)
 
@@ -252,9 +252,9 @@
     for load in loads:
         load.start()
     inverse = w[...]
-    for _ in range(3):
+    for _ in range(2):
         error = jnp.where(near[:1, :1] > 0, tri_half(residual(inverse, a[...], HI)), 0.0)
-        inverse = inverse - mm(error, inverse, NN, HI)
+        inverse = inverse - mm(error, inverse)
     inverse = inverse * across[:1]
     high = inverse.astype(bf16)
     low = (inverse - high.astype(f32)).astype(bf16)
@@ -280,12 +280,12 @@
     sqz[g, z] = line
     sq[...] = line
     got_sq = [send(sq, sqz.at[g, z], s_sq, k, at.up(k)) for k in upwards]
+    arrived(got_l)
+    got_lz = send_line(lambda other: oth.at[x, z], lambda place: oth.at[x, place], s_lz, at)
     got_rh = [send(rh.at[r], rh.at[r], s_rh, k, at.at(row=d)) for k, d in enumerate(at.row)]
     arrived(got_tl)
     tls[...] = (tl[r] + jnp.sum(rtl[...].astype(f32), axis=0)).astype(bf16)
     got_to = [send(tls, tlo, s_to, 0, at.at(g=o))]
-    arrived(got_l)
-    got_lz = send_line(lambda other: oth.at[x, z], lambda place: oth.at[x, place], s_lz, at)
     arrived(got_sh)
     got_ro = [send(rho.at[r], rho.at[r], s_ro, k, at.at(row=d)) for k, d in enumerate(at.row)]
     arrived(got_sq)
@@ -400,7 +400,7 @@
             pairs(nr - 1), pairs(nx - 1), pairs(nz), pairs(nz), pairs(nx - 1), pairs(part - 1), pairs(part - 1),
             pairs(nr - 1),
         ],
-        (mom, grad, fq, weights, tokens), 0, limit=52.3,
+        [pltpu.with_memory_space_constraint(a, pltpu.HBM) for a in (mom, grad, fq, weights, tokens)], 0,
     )
     square = ((RANK, RANK), f32, "v")
     start = call(

time: 140 us -> 138 us (0.986)
  local copies, waits for them, and re-layouts: 1.8 us -> 0.02 us
    unnamed x10 -> x8, local copies, waits for them, and re-layouts: 1.8 us -> 0.02 us
where the time goes in v6:
time: 138 us
  Pallas kernels  137 us (99%)
    pallas_call x4, Pallas kernels, call(): pl.pallas_call(kernel, out_shape=[jax.ShapeDtypeStruct(s, t) for s, t, _...  137 us

profile of v6, /device:TPU:1, one launch (start us, length us, event | category | flops | bytes accessed | tf_op | source)
XLA Modules:
  0.0 138.1 jit_solution(7215484461189818377)
XLA Ops:
  0.6 0.0 copy-start.1
  0.6 0.0 copy-start.2
  0.7 0.0 copy-start.3
  0.7 49.9 %shard_map.84 = (bf16[512,256]{1,0:T(8,128)(2,1)S(1)}, f32[264,128]{1,0:T(8,128)S(1)}, f32[2,32,256]{2,1,0:T(8,128)S(1)}, bf16[512,512]{1,0:T(8,128)(2,1)S(1)}) custom-call(f32[512,512]{1,0:T(8,128)} %bitcast.9, bf16[512,512]{1,0:T(8,128)(2,1)} %bitcast.11, f32[32,512]{1,0:T(8,128)} %bitcast.13, f32[2,512,256]{2,1,0:T(8,128)} %w.1, bf16[256,512]{1,0:T(8,128)(2,1)} %tok.1), custom_call_target="tpu_custom_call" | custom-call | tf_op jit(solution)/shard_map/pallas_call | solution.py:367
  50.6 56.8 %shard_map.85 = (f32[256,256]{1,0:T(8,128)S(1)}, f32[256,256]{1,0:T(8,128)S(1)}, f32[8,256]{1,0:T(8,128)S(1)}, f32[8,128]{1,0:T(8,128)S(1)}) custom-call(f32[264,128]{1,0:T(8,128)S(1)} %get-tuple-element.26.packed), custom_call_target="tpu_custom_call" | custom-call | tf_op jit(solution)/shard_map/pallas_call | solution.py:367
  107.5 0.0 copy-done.1
  107.5 0.0 copy-done.2
  107.5 0.0 copy-done.3
  107.5 0.0 copy-start
  107.5 28.5 %shard_map.86 = (f32[512,512]{1,0:T(8,128)S(1)}, bf16[512,256]{1,0:T(8,128)(2,1)S(1)}, bf16[512,256]{1,0:T(8,128)(2,1)S(1)}, bf16[256,512]{1,0:T(8,128)(2,1)S(1)...) custom-call(bf16[512,512]{1,0:T(8,128)(2,1)S(1)} %get-tuple-element., ...), custom_call_target="tpu_custom_call" | custom-call | tf_op jit(solution)/shard_map/pallas_call | solution.py:367
  136.0 0.0 copy-done
  136.0 2.0 %shard_map.87 = (f32[512,512]{1,0:T(8,128)}, f32[2,512,256]{2,1,0:T(8,128)}, f32[32,512]{1,0:T(8,128)}, bf16[32,256]{1,0:T(8,128)(2,1)}) custom-call(f32[512,512]{1,0:T(8,128)S(1)} %get-tuple-element.31.mom, f32[2,512,256]{2,1,0:T(8,128)S(1)} %copy-done, f32[2,32,256]{2,1,0:T(8,128)S(1)} %get-tuple-element.32.base, ...), custom_call_target="tpu_custom_call" | custom-call | tf_op jit(solution)/shard_map/pallas_call | solution.py:367
Async XLA Ops:
  0.6 106.8 %copy-start.1 = (f32[1,512,512]{2,1,0:T(8,128)S(1)}, f32[1,512,512]{2,1,0:T(8,128)}, u32[]{:S(2)}) copy-start(f32[1,512,512]{2,1,0:T(8,128)} %param.5) | copy-start | bytes 3145732
  0.6 106.8 %copy-start.2 = (bf16[1,512,512]{2,1,0:T(8,128)(2,1)S(1)}, bf16[1,512,512]{2,1,0:T(8,128)(2,1)}, u32[]{:S(2)}) copy-start(bf16[1,512,512]{2,1,0:T(8,128)(2,1)} %param.6) | copy-start | bytes 1572868
  0.7 106.8 %copy-start.3 = (bf16[256,512]{1,0:T(8,128)(2,1)S(1)}, bf16[256,512]{1,0:T(8,128)(2,1)}, u32[]{:S(2)}) copy-start(bf16[256,512]{1,0:T(8,128)(2,1)} %tok.1) | copy-start | bytes 786436
  107.5 28.6 %copy-start = (f32[2,512,256]{2,1,0:T(8,128)S(1)}, f32[2,512,256]{2,1,0:T(8,128)}, u32[]{:S(2)}) copy-start(f32[2,512,256]{2,1,0:T(8,128)} %w.1) | copy-start | bytes 3145732

commit v7 on v5

--- a/solution.py
+++ b/solution.py
@@ -16,7 +16,7 @@
 EPSILON = 1e-06
 STEP = 0.4 * math.sqrt(max(D, HID))
 CHUNKS = 4
-NEAR = 0.16
+NEAR = 0.1
 NX = 4
 
 f32, bf16 = jnp.float32, jnp.bfloat16
@@ -209,8 +209,8 @@
     across_o[...] = jnp.broadcast_to(across, across_o.shape)
     w = eye - tri_half(jnp.where(i == j, 0.0, a))
     w = w - mm(tri_half(residual(w, a)), w)
-    w_o[...] = w
     e = residual(w, a)
+    w_o[...] = w - mm(tri_half(e), w)
     far = jnp.sum(e * e)
     near_o[...] = jnp.ones(near_o.shape, f32)
 
@@ -252,9 +252,9 @@
     for load in loads:
         load.start()
     inverse = w[...]
-    for _ in range(3):
+    for _ in range(2):
         error = jnp.where(near[:1, :1] > 0, tri_half(residual(inverse, a[...], HI)), 0.0)
-        inverse = inverse - mm(error, inverse, NN, HI)
+        inverse = inverse - mm(error, inverse)
     inverse = inverse * across[:1]
     high = inverse.astype(bf16)
     low = (inverse - high.astype(f32)).astype(bf16)

time: 139 us -> 139 us (level)
  no operation moved by 1% of the time
where the time goes in v7:
time: 139 us
  Pallas kernels  138 us (99%)
    pallas_call x4, Pallas kernels, call(): pl.pallas_call(kernel, out_shape=[jax.ShapeDtypeStruct(s, t) for s, t, _...  138 us

profile of v7, /device:TPU:1, one launch (start us, length us, event | category | flops | bytes accessed | tf_op | source)
XLA Modules:
  0.0 138.7 jit_solution(17934905005548611617)
XLA Ops:
  0.6 0.0 copy-start.1
  0.6 0.0 copy-start.2
  0.7 0.0 copy-start.3
  0.7 49.9 %shard_map.84 = (bf16[512,256]{1,0:T(8,128)(2,1)S(1)}, f32[264,128]{1,0:T(8,128)S(1)}, f32[2,32,256]{2,1,0:T(8,128)S(1)}, bf16[512,512]{1,0:T(8,128)(2,1)S(1)}) custom-call(f32[512,512]{1,0:T(8,128)} %bitcast.9, bf16[512,512]{1,0:T(8,128)(2,1)} %bitcast.11, f32[32,512]{1,0:T(8,128)} %bitcast.13, f32[2,512,256]{2,1,0:T(8,128)} %w.1, bf16[256,512]{1,0:T(8,128)(2,1)} %tok.1), custom_call_target="tpu_custom_call" | custom-call | tf_op jit(solution)/shard_map/pallas_call | solution.py:364
  50.6 56.8 %shard_map.85 = (f32[256,256]{1,0:T(8,128)S(1)}, f32[256,256]{1,0:T(8,128)S(1)}, f32[8,256]{1,0:T(8,128)S(1)}, f32[8,128]{1,0:T(8,128)S(1)}) custom-call(f32[264,128]{1,0:T(8,128)S(1)} %get-tuple-element.26.packed), custom_call_target="tpu_custom_call" | custom-call | tf_op jit(solution)/shard_map/pallas_call | solution.py:364
  107.5 0.0 copy-done.1
  107.5 0.0 copy-done.2
  107.5 0.0 copy-done.3
  107.5 0.0 copy-start
  107.5 29.1 %shard_map.86 = (f32[512,512]{1,0:T(8,128)S(1)}, bf16[512,256]{1,0:T(8,128)(2,1)S(1)}, bf16[512,256]{1,0:T(8,128)(2,1)S(1)}, bf16[256,512]{1,0:T(8,128)(2,1)S(1)...) custom-call(bf16[512,512]{1,0:T(8,128)(2,1)S(1)} %get-tuple-element., ...), custom_call_target="tpu_custom_call" | custom-call | tf_op jit(solution)/shard_map/pallas_call | solution.py:364
  136.6 0.0 copy-done
  136.6 2.0 %shard_map.87 = (f32[512,512]{1,0:T(8,128)}, f32[2,512,256]{2,1,0:T(8,128)}, f32[32,512]{1,0:T(8,128)}, bf16[32,256]{1,0:T(8,128)(2,1)}) custom-call(f32[512,512]{1,0:T(8,128)S(1)} %get-tuple-element.31.mom, f32[2,512,256]{2,1,0:T(8,128)S(1)} %copy-done, f32[2,32,256]{2,1,0:T(8,128)S(1)} %get-tuple-element.32.base, ...), custom_call_target="tpu_custom_call" | custom-call | tf_op jit(solution)/shard_map/pallas_call | solution.py:364
Async XLA Ops:
  0.6 106.8 %copy-start.1 = (f32[1,512,512]{2,1,0:T(8,128)S(1)}, f32[1,512,512]{2,1,0:T(8,128)}, u32[]{:S(2)}) copy-start(f32[1,512,512]{2,1,0:T(8,128)} %param.5) | copy-start | bytes 3145732
  0.6 106.8 %copy-start.2 = (bf16[1,512,512]{2,1,0:T(8,128)(2,1)S(1)}, bf16[1,512,512]{2,1,0:T(8,128)(2,1)}, u32[]{:S(2)}) copy-start(bf16[1,512,512]{2,1,0:T(8,128)(2,1)} %param.6) | copy-start | bytes 1572868
  0.7 106.8 %copy-start.3 = (bf16[256,512]{1,0:T(8,128)(2,1)S(1)}, bf16[256,512]{1,0:T(8,128)(2,1)}, u32[]{:S(2)}) copy-start(bf16[256,512]{1,0:T(8,128)(2,1)} %tok.1) | copy-start | bytes 786436
  107.5 29.1 %copy-start = (f32[2,512,256]{2,1,0:T(8,128)S(1)}, f32[2,512,256]{2,1,0:T(8,128)}, u32[]{:S(2)}) copy-start(f32[2,512,256]{2,1,0:T(8,128)} %w.1) | copy-start | bytes 3145732

commit v8 on v6

--- a/solution.py
+++ b/solution.py
@@ -280,12 +280,12 @@
     sqz[g, z] = line
     sq[...] = line
     got_sq = [send(sq, sqz.at[g, z], s_sq, k, at.up(k)) for k in upwards]
-    arrived(got_l)
-    got_lz = send_line(lambda other: oth.at[x, z], lambda place: oth.at[x, place], s_lz, at)
     got_rh = [send(rh.at[r], rh.at[r], s_rh, k, at.at(row=d)) for k, d in enumerate(at.row)]
     arrived(got_tl)
     tls[...] = (tl[r] + jnp.sum(rtl[...].astype(f32), axis=0)).astype(bf16)
     got_to = [send(tls, tlo, s_to, 0, at.at(g=o))]
+    arrived(got_l)
+    got_lz = send_line(lambda other: oth.at[x, z], lambda place: oth.at[x, place], s_lz, at)
     arrived(got_sh)
     got_ro = [send(rho.at[r], rho.at[r], s_ro, k, at.at(row=d)) for k, d in enumerate(at.row)]
     arrived(got_sq)

time: 138 us -> 139 us (level)
  no operation moved by 1% of the time
where the time goes in v8:
time: 139 us
  Pallas kernels  138 us (99%)
    pallas_call x4, Pallas kernels, call(): pl.pallas_call(kernel, out_shape=[jax.ShapeDtypeStruct(s, t) for s, t, _...  138 us

profile of v8, /device:TPU:1, one launch (start us, length us, event | category | flops | bytes accessed | tf_op | source)
XLA Modules:
  0.0 139.0 jit_solution(12679101631079670991)
XLA Ops:
  0.6 0.0 copy-start.1
  0.6 0.0 copy-start.2
  0.7 0.0 copy-start.3
  0.7 49.9 %shard_map.84 = (bf16[512,256]{1,0:T(8,128)(2,1)S(1)}, f32[264,128]{1,0:T(8,128)S(1)}, f32[2,32,256]{2,1,0:T(8,128)S(1)}, bf16[512,512]{1,0:T(8,128)(2,1)S(1)}) custom-call(f32[512,512]{1,0:T(8,128)} %bitcast.9, bf16[512,512]{1,0:T(8,128)(2,1)} %bitcast.11, f32[32,512]{1,0:T(8,128)} %bitcast.13, f32[2,512,256]{2,1,0:T(8,128)} %w.1, bf16[256,512]{1,0:T(8,128)(2,1)} %tok.1), custom_call_target="tpu_custom_call" | custom-call | tf_op jit(solution)/shard_map/pallas_call | solution.py:367
  50.6 56.8 %shard_map.85 = (f32[256,256]{1,0:T(8,128)S(1)}, f32[256,256]{1,0:T(8,128)S(1)}, f32[8,256]{1,0:T(8,128)S(1)}, f32[8,128]{1,0:T(8,128)S(1)}) custom-call(f32[264,128]{1,0:T(8,128)S(1)} %get-tuple-element.26.packed), custom_call_target="tpu_custom_call" | custom-call | tf_op jit(solution)/shard_map/pallas_call | solution.py:367
  107.5 0.0 copy-done.1
  107.5 0.0 copy-done.2
  107.5 0.0 copy-done.3
  107.5 0.0 copy-start
  107.5 29.4 %shard_map.86 = (f32[512,512]{1,0:T(8,128)S(1)}, bf16[512,256]{1,0:T(8,128)(2,1)S(1)}, bf16[512,256]{1,0:T(8,128)(2,1)S(1)}, bf16[256,512]{1,0:T(8,128)(2,1)S(1)...) custom-call(bf16[512,512]{1,0:T(8,128)(2,1)S(1)} %get-tuple-element., ...), custom_call_target="tpu_custom_call" | custom-call | tf_op jit(solution)/shard_map/pallas_call | solution.py:367
  136.9 0.0 copy-done
  136.9 2.0 %shard_map.87 = (f32[512,512]{1,0:T(8,128)}, f32[2,512,256]{2,1,0:T(8,128)}, f32[32,512]{1,0:T(8,128)}, bf16[32,256]{1,0:T(8,128)(2,1)}) custom-call(f32[512,512]{1,0:T(8,128)S(1)} %get-tuple-element.31.mom, f32[2,512,256]{2,1,0:T(8,128)S(1)} %copy-done, f32[2,32,256]{2,1,0:T(8,128)S(1)} %get-tuple-element.32.base, ...), custom_call_target="tpu_custom_call" | custom-call | tf_op jit(solution)/shard_map/pallas_call | solution.py:367
Async XLA Ops:
  0.6 106.8 %copy-start.1 = (f32[1,512,512]{2,1,0:T(8,128)S(1)}, f32[1,512,512]{2,1,0:T(8,128)}, u32[]{:S(2)}) copy-start(f32[1,512,512]{2,1,0:T(8,128)} %param.5) | copy-start | bytes 3145732
  0.6 106.8 %copy-start.2 = (bf16[1,512,512]{2,1,0:T(8,128)(2,1)S(1)}, bf16[1,512,512]{2,1,0:T(8,128)(2,1)}, u32[]{:S(2)}) copy-start(bf16[1,512,512]{2,1,0:T(8,128)(2,1)} %param.6) | copy-start | bytes 1572868
  0.7 106.8 %copy-start.3 = (bf16[256,512]{1,0:T(8,128)(2,1)S(1)}, bf16[256,512]{1,0:T(8,128)(2,1)}, u32[]{:S(2)}) copy-start(bf16[256,512]{1,0:T(8,128)(2,1)} %tok.1) | copy-start | bytes 786436
  107.5 29.4 %copy-start = (f32[2,512,256]{2,1,0:T(8,128)S(1)}, f32[2,512,256]{2,1,0:T(8,128)}, u32[]{:S(2)}) copy-start(f32[2,512,256]{2,1,0:T(8,128)} %w.1) | copy-start | bytes 3145732

commit v9 on v6

--- a/solution.py
+++ b/solution.py
@@ -270,16 +270,16 @@
     got_tl = [send(tlb.at[at.rs[d]], rtl.at[k], s_tl, k, at.at(row=d)) for k, d in enumerate(at.row)]
     arrived(got_rt)
     share = rt[r] + jnp.sum(rrt[...].astype(f32), axis=0)
-    share_o[...] = share
-    rh[r] = share.astype(bf16)
-    sho[...] = share_o[:, pl.ds(pl.multiple_of(o * half, half), half)].astype(bf16)
-    got_sh = [send(sho, rho.at[r], s_sh, 0, at.at(g=o))]
     eye = lax.broadcasted_iota(jnp.int32, (kr, 128), 0) == lax.broadcasted_iota(jnp.int32, (kr, 128), 1)
     squares = jnp.sum(share * share, axis=1, keepdims=True)
     line = jnp.sum(jnp.where(eye, squares, 0.0), axis=0, keepdims=True)
     sqz[g, z] = line
     sq[...] = line
     got_sq = [send(sq, sqz.at[g, z], s_sq, k, at.up(k)) for k in upwards]
+    share_o[...] = share
+    rh[r] = share.astype(bf16)
+    sho[...] = share_o[:, pl.ds(pl.multiple_of(o * half, half), half)].astype(bf16)
+    got_sh = [send(sho, rho.at[r], s_sh, 0, at.at(g=o))]
     arrived(got_l)
     got_lz = send_line(lambda other: oth.at[x, z], lambda place: oth.at[x, place], s_lz, at)
     got_rh = [send(rh.at[r], rh.at[r], s_rh, k, at.at(row=d)) for k, d in enumerate(at.row)]

time: 138 us -> 137 us (level)
  no operation moved by 1% of the time
where the time goes in v9:
time: 137 us
  Pallas kernels  136 us (99%)
    pallas_call x4, Pallas kernels, call(): pl.pallas_call(kernel, out_shape=[jax.ShapeDtypeStruct(s, t) for s, t, _...  136 us

profile of v9, /device:TPU:1, one launch (start us, length us, event | category | flops | bytes accessed | tf_op | source)
XLA Modules:
  0.0 137.2 jit_solution(10778297926912794240)
XLA Ops:
  0.6 0.0 copy-start.1
  0.6 0.0 copy-start.2
  0.7 0.0 copy-start.3
  0.7 49.9 %shard_map.84 = (bf16[512,256]{1,0:T(8,128)(2,1)S(1)}, f32[264,128]{1,0:T(8,128)S(1)}, f32[2,32,256]{2,1,0:T(8,128)S(1)}, bf16[512,512]{1,0:T(8,128)(2,1)S(1)}) custom-call(f32[512,512]{1,0:T(8,128)} %bitcast.9, bf16[512,512]{1,0:T(8,128)(2,1)} %bitcast.11, f32[32,512]{1,0:T(8,128)} %bitcast.13, f32[2,512,256]{2,1,0:T(8,128)} %w.1, bf16[256,512]{1,0:T(8,128)(2,1)} %tok.1), custom_call_target="tpu_custom_call" | custom-call | tf_op jit(solution)/shard_map/pallas_call | solution.py:367
  50.6 56.8 %shard_map.85 = (f32[256,256]{1,0:T(8,128)S(1)}, f32[256,256]{1,0:T(8,128)S(1)}, f32[8,256]{1,0:T(8,128)S(1)}, f32[8,128]{1,0:T(8,128)S(1)}) custom-call(f32[264,128]{1,0:T(8,128)S(1)} %get-tuple-element.26.packed), custom_call_target="tpu_custom_call" | custom-call | tf_op jit(solution)/shard_map/pallas_call | solution.py:367
  107.5 0.0 copy-done.1
  107.5 0.0 copy-done.2
  107.5 0.0 copy-done.3
  107.5 0.0 copy-start
  107.5 27.6 %shard_map.86 = (f32[512,512]{1,0:T(8,128)S(1)}, bf16[512,256]{1,0:T(8,128)(2,1)S(1)}, bf16[512,256]{1,0:T(8,128)(2,1)S(1)}, bf16[256,512]{1,0:T(8,128)(2,1)S(1)...) custom-call(bf16[512,512]{1,0:T(8,128)(2,1)S(1)} %get-tuple-element., ...), custom_call_target="tpu_custom_call" | custom-call | tf_op jit(solution)/shard_map/pallas_call | solution.py:367
  135.1 0.0 copy-done
  135.1 2.0 %shard_map.87 = (f32[512,512]{1,0:T(8,128)}, f32[2,512,256]{2,1,0:T(8,128)}, f32[32,512]{1,0:T(8,128)}, bf16[32,256]{1,0:T(8,128)(2,1)}) custom-call(f32[512,512]{1,0:T(8,128)S(1)} %get-tuple-element.31.mom, f32[2,512,256]{2,1,0:T(8,128)S(1)} %copy-done, f32[2,32,256]{2,1,0:T(8,128)S(1)} %get-tuple-element.32.base, ...), custom_call_target="tpu_custom_call" | custom-call | tf_op jit(solution)/shard_map/pallas_call | solution.py:367
Async XLA Ops:
  0.6 106.8 %copy-start.1 = (f32[1,512,512]{2,1,0:T(8,128)S(1)}, f32[1,512,512]{2,1,0:T(8,128)}, u32[]{:S(2)}) copy-start(f32[1,512,512]{2,1,0:T(8,128)} %param.5) | copy-start | bytes 3145732
  0.6 106.8 %copy-start.2 = (bf16[1,512,512]{2,1,0:T(8,128)(2,1)S(1)}, bf16[1,512,512]{2,1,0:T(8,128)(2,1)}, u32[]{:S(2)}) copy-start(bf16[1,512,512]{2,1,0:T(8,128)(2,1)} %param.6) | copy-start | bytes 1572868
  0.7 106.8 %copy-start.3 = (bf16[256,512]{1,0:T(8,128)(2,1)S(1)}, bf16[256,512]{1,0:T(8,128)(2,1)}, u32[]{:S(2)}) copy-start(bf16[256,512]{1,0:T(8,128)(2,1)} %tok.1) | copy-start | bytes 786436
  107.5 27.6 %copy-start = (f32[2,512,256]{2,1,0:T(8,128)S(1)}, f32[2,512,256]{2,1,0:T(8,128)}, u32[]{:S(2)}) copy-start(f32[2,512,256]{2,1,0:T(8,128)} %w.1) | copy-start | bytes 3145732
